TPU v7x, 512 devices: a whole 4x8x8 slice. The times are simulated.
512 devices in a mesh: kb: 32 (over z, y_lo), vir: 16 (over x, y_hi, core).
Axes of the slice: x: 4, y: 8 (y_hi: 2, y_lo: 4; y = y_hi * 4 + y_lo), z: 8, core: 2. Of those that a mesh axis runs over, the one named last changes fastest.
Arguments:
- amps: bfloat16 [32, 120, 160, 160], P('kb', None, 'vir'), may hold values from -6 to 6
- ints_pair: bfloat16 [64, 160, 16, 160], P('kb', None, None, 'vir'), may hold values from -0.5 to 0.5
- ints_fold: bfloat16 [64, 16, 160, 160], P('kb'), may hold values from -0.125 to 0.125
- eps_occ: float32 [64, 16], replicated, may hold values from -2 to -0.3
- eps_vir: float32 [64, 160], replicated, may hold values from 0.3 to 3
- kconserve: int32 [64, 64], replicated, may hold values from 0 to 63, as said below
- plan: int32 [2], replicated, may hold values from 0 to 63
Outputs:
- residual: bfloat16 [32, 120, 160, 160], P('kb', None, 'vir')
Inputs may be any that keep to these rules, and one draw needn't show every extreme that they name: kconserve[k1, k3] labels the mesh point of momentum k1 - k3 modulo the 4 x 4 x 4 mesh under a labelling of the points drawn from the seed; each row and each column is a permutation.
All inputs are finite; a program needn't handle non-finite values.
Results may differ from a plain program's by a relative error of at most 0.0049.
Values may be sent and summed in bfloat16 or wider, within the bound.
A program may use at most 64 MiB of HBM per device.

v0:
```python
import jax
import jax.numpy as jnp
import numpy as np
from jax import lax
from jax.sharding import PartitionSpec as P

STEPS = 2


def broadcast(block, axis, source):
    block = jnp.where(lax.axis_index(axis) == source, block, jnp.zeros_like(block))
    return lax.psum(block, axis)


def local(amps, ints_pair, ints_fold, eps_occ, eps_vir, kconserve, plan):
    kdev = ints_pair.shape[0]
    vloc = amps.shape[2]
    width = amps.shape[3]
    occ_n = ints_pair.shape[2]
    pair_n = amps.shape[1]
    first_idx, second_idx = np.triu_indices(occ_n, 1)
    kfirst = lax.axis_index("kb") * kdev
    vstart = lax.axis_index("vir") * vloc
    occ_first = lax.dynamic_index_in_dim(eps_occ, kfirst, 0, keepdims=False)
    vir_first = lax.dynamic_index_in_dim(eps_vir, kfirst, 0, keepdims=False)
    vir_local = lax.dynamic_slice_in_dim(vir_first, vstart, vloc)
    pair_eps = occ_first[first_idx] + occ_first[second_idx]
    left_den = (vir_local[None, :] - pair_eps[:, None]).reshape(pair_n * vloc, 1)
    rows = amps[0].reshape(pair_n * vloc, width)
    total = jnp.zeros((pair_n * vloc, width), jnp.float32)
    for step in range(STEPS):
        kthird = plan[step]
        owner = kthird // kdev
        slot = kthird % kdev
        pair_slot = lax.dynamic_index_in_dim(ints_pair, slot, 0, keepdims=False)
        fold_slot = lax.dynamic_index_in_dim(ints_fold, slot, 0, keepdims=False)
        pair_got, fold_full = (broadcast(pair_slot, "kb", owner), broadcast(fold_slot, "kb", owner))
        pair_full = lax.all_gather(pair_got, "vir", axis=2, tiled=True)
        zeta = jnp.dot(
            rows, pair_full.reshape(width, occ_n * width), preferred_element_type=jnp.float32
        )
        ksecond = kconserve[kfirst, kthird]
        vir_second = lax.dynamic_index_in_dim(eps_vir, ksecond, 0, keepdims=False)
        occ_third = lax.dynamic_index_in_dim(eps_occ, kthird, 0, keepdims=False)
        right_den = (vir_second[None, :] - occ_third[:, None]).reshape(1, occ_n * width)
        triples = (zeta / (left_den + right_den)).astype(jnp.bfloat16)
        total = total + jnp.dot(
            triples, fold_full.reshape(occ_n * width, width), preferred_element_type=jnp.float32
        )
    return total.reshape(1, pair_n, vloc, width).astype(jnp.bfloat16)


def solution(mesh):
    return jax.shard_map(
        local,
        mesh=mesh,
        in_specs=(
            P("kb", None, "vir", None),
            P("kb", None, None, "vir"),
            P("kb", None, None, None),
            P(),
            P(),
            P(),
            P(),
        ),
        out_specs=P("kb", None, "vir", None),
        check_vma=False,
    )
```

profile of v0, /device:TPU:8, one launch (start us, length us, event | category | flops | bytes accessed | tf_op | source)
XLA Modules:
  0.0 668.1 jit_solution(619398095134979531)
XLA Ops:
  6.5 1.4 fusion.4
  13.0 1.6 select_bitcast_fusion
  14.7 0.0 all-reduce.5.cloned.1.call-update
  14.7 0.0 all-reduce.7.cloned.1.call-start
  14.7 3.5 dynamic-slice_select_fusion
  20.9 1.4 fusion.2
  24.8 0.2 dynamic-slice_reduce_fusion
  26.3 0.7 constant_dynamic-slice_fusion.1
  27.0 0.1 broadcast_subtract_fusion.2
  27.4 1.4 copy.19
  28.8 1.2 reshape_squeeze.3
  30.0 0.1 sub.88
  30.1 0.7 fusion.3
  30.8 0.8 dynamic-slice_bitcast_fusion
  31.9 10.0 %select_add_fusion = f32[120]{0:T(128)S(1)} fusion(pred[120]{0:T(512)(128)(4,1)S(1)} %copy-done.4, pred[120]{0:T(512)(128)(4,1)S(1)} %copy-done.5, pred[120]{0:T(512)(128)(4,1)S(1)} %copy-done.6, pred[120]{0:T(512)(128)(4,1)S(1)} %copy-done.7, pred[120]{0:T(512)(128)(4,1)S(1)} %copy-done.8, pred[120]{0:T(512)(128)(4,1)S(1)} %copy-done.9, ...), kind=kLoop, calls=%fused_computation.19 | loop fusion | flops 3480 | bytes 3904 | tf_op jit(solution)/shard_map/add | solution.py:27
  41.9 0.1 broadcast_subtract_fusion
  42.0 0.1 sub.82
  42.2 0.1 broadcast_subtract_fusion.1
  42.2 0.1 sub.95
  42.3 264.2 %all-reduce.5.cloned.1.call-done = (bf16[160,16,10]{0,1,2:T(8,128)(2,1)}, bf16[160,16,10]{0,1,2:T(8,128)(2,1)}) async-done(((bf16[160,16,10]{0,1,2:T(8,128)(2,1)}, bf16[160,16,10]{0,1,2:T(8,128)(2,1)}), (bf16[160,16,10]{0,1,2:T(8,128)(2,1)}, bf16[160,16,10]{0,1,2:T(8,128)(2,1)})) %all-reduce.5.cloned.1.call-update) | async-done | bytes 102416 | tf_op jit(solution)/shard_map/psum | solution.py:12
  306.6 52.7 %all_gather.6 = bf16[160,16,160]{0,1,2:T(8,128)(2,1)S(1)} all-gather(bf16[160,16,10]{0,1,2:T(8,128)(2,1)} %get-tuple-element.7), channel_id=1, replica_groups=mesh['kb'=32,'vir'=16] {'vir'}, dimensions={2}, use_global_device_ids=true | all-gather | bytes 870400 | tf_op jit(solution)/shard_map/all_gather | solution.py:38
  359.3 1.9 copy.18
  361.2 2.0 reshape.94
  363.2 56.0 %all_gather.7 = bf16[160,16,160]{0,1,2:T(8,128)(2,1)S(1)} all-gather(bf16[160,16,10]{0,1,2:T(8,128)(2,1)S(1)} %copy-done.2), channel_id=1, replica_groups=mesh['kb'=32,'vir'=16] {'vir'}, dimensions={2}, use_global_device_ids=true | all-gather | bytes 870400 | tf_op jit(solution)/shard_map/all_gather | solution.py:38
  419.3 1.9 copy.20
  421.2 2.0 reshape.96
  423.1 226.2 %all-reduce.7.cloned.1.call-done = (bf16[2560,160]{1,0:T(8,128)(2,1)}, bf16[2560,160]{1,0:T(8,128)(2,1)}) async-done(((bf16[2560,160]{1,0:T(8,128)(2,1)}, bf16[2560,160]{1,0:T(8,128)(2,1)}), (bf16[2560,160]{1,0:T(8,128)(2,1)}, bf16[2560,160]{1,0:T(8,128)(2,1)})) %all-reduce.7.cloned.1.call-update) | async-done | bytes 1638416 | tf_op jit(solution)/shard_map/psum | solution.py:12
  649.3 5.1 fusion.1
  654.5 4.9 fusion
  659.4 0.2 copy.21
  659.6 0.3 convert_element_type.23
  659.9 1.4 copy.22
  (66 shorter events, 0.2 us)
Async XLA Ops:
  6.5 300.0 %all-reduce.5.cloned.1.call-start = ((), (), s32[]{:S(2)}) async-start(), calls=%async_computation | async-start | bytes 327680 | tf_op jit(solution)/shard_map/psum | solution.py:12
  14.7 634.6 %all-reduce.7.cloned.1.call-start = ((), (), s32[]{:S(2)}) async-start(), calls=%async_computation.1 | async-start | bytes 5242880 | tf_op jit(solution)/shard_map/psum | solution.py:12
  18.3 6.5 copy-start.3
  18.3 8.8 %copy-start.1 = (bf16[1,120,10,160]{1,3,2,0:T(8,128)(2,1)S(1)}, bf16[1,120,10,160]{1,3,2,0:T(8,128)(2,1)}, u32[]{:S(2)}) copy-start(bf16[1,120,10,160]{1,3,2,0:T(8,128)(2,1)} %param.11) | copy-start | bytes 1152004
  27.1 4.5 copy-start.4
  27.1 4.5 copy-start.5
  27.1 4.5 copy-start.6
  27.1 4.5 copy-start.7
  27.1 4.5 copy-start.8
  27.1 4.5 copy-start.9
  27.2 4.5 copy-start.10
  27.2 4.5 copy-start.11
  27.2 4.5 copy-start.12
  27.2 4.5 copy-start.13
  27.2 4.5 copy-start.14
  27.2 4.5 copy-start.15
  27.2 4.5 copy-start.16
  27.2 4.5 copy-start.17
  27.3 4.5 copy-start.18
  27.3 4.5 copy-start.19
  27.3 4.5 copy-start.20
  27.3 4.5 copy-start.21
  27.3 4.5 copy-start.22
  27.3 4.5 copy-start.23
  27.3 4.5 copy-start.24
  27.3 4.5 copy-start.25
  27.4 4.5 copy-start.26
  27.4 4.5 copy-start.27
  27.4 4.5 copy-start.28
  27.4 4.5 copy-start.29
  27.4 4.5 copy-start.30
  649.3 5.1 copy-start
  (2 other events, 6.5 us)
Sparse Core Ops, SparseCore 0:
  14.8 291.7 all-reduce.4
  309.8 339.4 all-reduce.6
where the time goes:
time: 669 us; the launch traced here: 668 us
  waiting for transfers between devices  490 us (73%)
  blocking collectives  109 us (16%)
  between operations  25.4 us (4%)
  local copies, waits for them, and re-layouts  18 us (3%)
  other arithmetic  15.5 us (2%)
  matrix products  10 us (1%)
    psum x2, waiting for transfers between devices, broadcast(): return lax.psum(block, axis)  490 us
    all_gather x2, blocking collectives, local(): pair_full = lax.all_gather(pair_got, 'vir', axis=2, tiled=True)  109 us
  transfers between devices with their start and end apart: 2, of which 2 were waited for; matrix products, arithmetic and copies ran while one was open for 4% of the time, Pallas kernels for 0%

commit v1 on v0

v1 whole, which is shorter than its diff:
```python
import functools

import jax
import jax.numpy as jnp
import numpy as np
from jax import lax
from jax.experimental import pallas as pl
from jax.experimental.pallas import tpu as pltpu
from jax.sharding import PartitionSpec as P

STEPS = 2
TILES = 25
MESH = pl.DeviceIdType.MESH
F32 = jnp.float32
BF16 = jnp.bfloat16
NT = (((1,), (1,)), ((), ()))
TN = (((0,), (0,)), ((), ()))


def iota(shape, dim):
    return lax.broadcasted_iota(jnp.int32, shape, dim)


def onehot(mask):
    return jnp.where(mask, 1.0, 0.0).astype(BF16)


def prep_kernel(plan, kcons, amps, pair, fold, occt, evir, x_out, l_out, left_out, right_out):
    kb = lax.axis_index("kb")
    vir = lax.axis_index("vir")
    kfirst = 2 * kb
    pick = onehot(
        (iota((160, 2560), 0) % 16 == iota((160, 2560), 1) // 160)
        & (iota((160, 2560), 1) % 160 == 10 * vir + iota((160, 2560), 0) // 16)
    )
    row, col = iota((160, 128), 0), iota((160, 128), 1)
    tail = [onehot((row - 128 == col - 32 * j) & (row >= 128)) for j in range(4)]
    dot = functools.partial(jnp.dot, preferred_element_type=F32)
    for s in range(STEPS):
        slot = plan[s] % 2
        p = pair[slot].reshape(5, 2, 16, 160)
        f = dot(pick, fold[slot].reshape(2560, 160)).astype(BF16).reshape(5, 2, 16, 160)
        parts = [p[:, 0], p[:, 1], f[:, 0], f[:, 1]]
        for j in range(4):
            x_out[5 * j:5 * j + 5, s] = parts[j][:, :, :128]
        flat = [q.reshape(80, 160) for q in (p[:, 0], f[:, 0], p[:, 1], f[:, 1])]
        rem = sum(dot(flat[j], tail[j]) for j in range(4))
        x_out[20:25, s] = rem.astype(BF16).reshape(5, 16, 128)
    l_out[...] = jnp.zeros_like(l_out)
    for q in range(2):
        place = onehot(
            iota((160, 256), 0) + jnp.where(iota((160, 256), 0) >= 128, 64 * q, 0) == iota((160, 256), 1)
        )
        for a in range(10):
            l_out[q, a, :120] = lax.dot_general(amps[a], place, TN, preferred_element_type=F32).astype(BF16)
    row = iota((128, 16), 0)
    band = iota((128, 16), 1)
    member = jnp.zeros((128, 16), jnp.bool_)
    start = 0
    for i in range(16):
        n = 15 - i
        inside = (row >= start) & (row < start + n)
        member = member | (inside & ((band == i) | (band == i + 1 + row - start)))
        start += n
    sums = jnp.dot(jnp.where(member, 1.0, 0.0), occt[...], precision=lax.Precision.HIGHEST, preferred_element_type=F32)
    pe = jnp.sum(jnp.where(iota((128, 64), 1) == kfirst, sums, 0.0), axis=1, keepdims=True)
    vrow = evir[pl.ds(kfirst, 1), :]
    for a in range(10):
        mine = jnp.sum(jnp.where(iota((1, 160), 1) == 10 * vir + a, vrow, 0.0), axis=1, keepdims=True)
        left_out[a] = jnp.broadcast_to(mine - pe, (128, 128))
    r = iota((24, 128), 0)
    lane = iota((24, 128), 1)
    rq, rp, rt = r // 10, (r // 5) % 2, r % 5
    v8 = lane // 16
    xx = jnp.where(rp == 0, v8 // 2, v8 % 4)
    yh = jnp.where(rp == 0, v8 % 2, v8 // 4)
    col = jnp.minimum(10 * ((xx * 2 + yh) * 2 + rp) + 2 * rt + rq, 159)
    occ16 = lax.dot_general(
        occt[...], jnp.where(iota((16, 128), 1) % 16 == iota((16, 128), 0), 1.0, 0.0), TN,
        precision=lax.Precision.HIGHEST, preferred_element_type=F32)
    for s in range(STEPS):
        k3 = plan[s]
        k2 = kcons[kfirst, k3]
        vs = evir[pl.ds(k2, 1), :]
        low = jnp.broadcast_to(vs[:, :128], (24, 128))
        high = jnp.broadcast_to(vs[:, 32:160], (24, 128))
        got = jnp.where(
            col < 128,
            jnp.take_along_axis(low, jnp.minimum(col, 127), axis=1),
            jnp.take_along_axis(high, jnp.maximum(col - 32, 0), axis=1),
        )
        occ = jnp.sum(jnp.where(iota((64, 128), 0) == k3, occ16, 0.0), axis=0, keepdims=True)
        right_out[s] = got - occ


def main_kernel(plan, x, l_ref, left, right, out,
                cand, buf, pq, fq, acc,
                s1, r1, s2, r2, s3, r3, s4, r4, s5, r5):
    kb = lax.axis_index("kb")
    vir = lax.axis_index("vir")
    z, yl = kb // 4, kb % 4
    xx, yh, core = vir // 4, (vir // 2) % 2, vir % 2
    y = yh * 4 + yl
    f = y + core * (z - y)
    l = z + core * (y - z)

    def dev(x_, f_, l_):
        y_ = f_ + core * (l_ - f_)
        z_ = l_ + core * (f_ - l_)
        return (z_ * 4 + y_ % 4, (x_ * 2 + y_ // 4) * 2 + core)

    sibling = (kb, vir + 1 - 2 * core)
    rnext = dev(xx, f, (l + 1) % 8)
    lnext = dev(xx, f, (l + 7) % 8)

    barrier = pltpu.get_barrier_semaphore()

    def greet(d):
        pl.semaphore_signal(barrier, inc=1, device_id=d, device_id_type=MESH)

    @pl.loop(1, 32)
    def _(i):
        greet(((kb + i) % 32, vir))

    @pl.loop(1, 8)
    def _(i):
        greet(dev(xx, (f + i) % 8, l))

    @pl.loop(1, 4)
    def _(i):
        greet(dev((xx + i) % 4, f, l))

    greet(rnext)
    greet(lnext)
    greet(sibling)
    pl.semaphore_wait(barrier, 31 + 7 + 3 + 2 + 1)

    def remote(src, dst, ss, rs, d):
        return pltpu.make_async_remote_copy(
            src_ref=src, dst_ref=dst, send_sem=ss, recv_sem=rs, device_id=d, device_id_type=MESH)

    def copy1(i, target, slot):
        return remote(x.at[target], cand.at[slot], s1.at[i], r1.at[i], (target, vir))

    @pl.loop(1, 32)
    def _(i):
        target = (kb + i) % 32

        @pl.when(target < TILES)
        def _():
            copy1(i, target, kb).start()

    @pl.when(kb < TILES)
    def _():
        cand[kb] = x[kb]

        @pl.loop(1, 32)
        def _(i):
            copy1(i, kb, (kb + 32 - i) % 32).wait_recv()

        for s in range(STEPS):
            buf[core, s, l, xx, f] = cand[plan[s] // 2, s]

    @pl.when(kb >= TILES)
    def _():
        for s in range(STEPS):
            buf[core, s, l, xx, f] = jnp.zeros((16, 128), BF16)

    def copy2(i, slot):
        here = buf.at[core, :, l, xx, slot]
        return remote(here, here, s2.at[i], r2.at[i], dev(xx, (f + i) % 8, l))

    @pl.loop(1, 8)
    def _(i):
        copy2(i, f).start()

    @pl.loop(1, 8)
    def _(i):
        copy2(i, (f + 8 - i) % 8).wait_recv()

    def copy3(s, i, slot):
        here = buf.at[core, s, l, slot]
        return remote(here, here, s3.at[s, i], r3.at[s, i], dev((xx + i) % 4, f, l))

    for s in range(STEPS):
        for i in range(1, 4):
            copy3(s, i, xx).start()

    def copy4(s, t, way, half, origin):
        here = buf.at[core, s, origin, pl.ds(2 * half, 2)]
        return remote(here, here, s4.at[s, t, way, half], r4.at[s, t, way, half], lnext if way else rnext)

    def copy5(s, plane, origin, half):
        here = buf.at[plane, s, origin, pl.ds(2 * half, 2)]
        return remote(here, here, s5.at[s, origin, half], r5.at[s, origin, half], sibling)

    def begin(s):
        for i in range(1, 4):
            copy3(s, i, (xx + 4 - i) % 4).wait_recv()
        for half in range(2):
            for way in range(2):
                copy4(s, 0, way, half, l).start()
        for half in range(2):
            copy5(s, core, l, half).start()

    def hop(s, t):
        for half in range(2):
            for way in range(2):
                if t == 4 and way != half:
                    continue
                origin = (l + t) % 8 if way else (l + 8 - t) % 8
                copy4(s, t - 1, way, half, origin).wait_recv()
                if t < 3 or (t == 3 and way == half):
                    copy4(s, t, way, half, origin).start()
                copy5(s, core, origin, half).start()

    def finish(s):
        for half in range(2):
            @pl.loop(0, 8)
            def _(o, half=half):
                copy5(s, 1 - core, o, half).wait_recv()

    def tiles(s, base):
        got = []
        for plane in range(2):
            for tp in range(5):
                g = base + tp
                zz, ll = g // 4, g % 4
                if plane == 0:
                    got += [buf[0, s, zz, a, b * 4 + ll] for a in range(4) for b in range(2)]
                else:
                    got += [buf[1, s, b * 4 + ll, a, zz] for b in range(2) for a in range(4)]
        return got

    def assemble(s, q):
        for i, tile in enumerate(tiles(s, 5 * q)):
            pq[16 * i:16 * i + 16, :128] = tile
        for i, tile in enumerate(tiles(s, 10 + 5 * q)):
            fq[16 * i:16 * i + 16, :128] = tile
        for i, tile in enumerate(tiles(s, 20)):
            pq[16 * i:16 * i + 16, 128:] = tile
            fq[16 * i:16 * i + 16, 128:] = tile

    def block(s, q, m):
        rows = l_ref[q, pl.ds(2 * m, 2)].reshape(256, 256)
        lf = left[pl.ds(2 * m, 2)].reshape(256, 128)
        parts = []
        for j in range(5):
            zeta = lax.dot_general(rows, pq[256 * j:256 * j + 256, :], NT, preferred_element_type=F32)
            for i in range(2):
                r = 10 * q + 2 * j + i
                den = lf + right[s, r:r + 1, :]
                parts.append((zeta[:, 128 * i:128 * i + 128] / den).astype(BF16))
        return jnp.dot(jnp.concatenate(parts, axis=1), fq[...], preferred_element_type=F32)

    begin(0)
    begin(1)
    for t in range(1, 5):
        hop(0, t)
    finish(0)
    for t in range(1, 5):
        hop(1, t)

    for q in range(2):
        assemble(0, q)

        @pl.loop(0, 5)
        def _(m, q=q):
            acc[q, m] = block(0, q, m)

    finish(1)
    assemble(1, 0)

    @pl.loop(0, 5)
    def _(m):
        acc[0, m] += block(1, 0, m)

    assemble(1, 1)
    row = iota((160, 256), 0)
    pick = onehot(row + jnp.where(row >= 128, 32, 0) == iota((160, 256), 1))

    @pl.loop(0, 5)
    def _(m):
        odd = acc[1, m] + block(1, 1, m)
        even = acc[0, m]
        total = jnp.concatenate(
            [even[:, :128] + odd[:, :128], even[:, 128:] + pltpu.roll(odd[:, 128:], 64, 1)], axis=1
        ).astype(BF16)
        done = lax.dot_general(pick, total, NT, preferred_element_type=F32).astype(BF16)
        out[2 * m] = done[:, :120]
        out[2 * m + 1] = done[:, 128:248]

    @pl.loop(1, 32)
    def _(i):
        target = (kb + i) % 32

        @pl.when(target < TILES)
        def _():
            copy1(i, target, kb).wait_send()

    @pl.loop(1, 8)
    def _(i):
        copy2(i, f).wait_send()

    for s in range(STEPS):
        for i in range(1, 4):
            copy3(s, i, xx).wait_send()
        for t in range(4):
            for half in range(2):
                for way in range(2):
                    if t == 3 and way != half:
                        continue
                    origin = (l + t) % 8 if way else (l + 8 - t) % 8
                    copy4(s, t, way, half, origin).wait_send()
        for half in range(2):
            @pl.loop(0, 8)
            def _(o, half=half, s=s):
                copy5(s, core, o, half).wait_send()


def local(amps, ints_pair, ints_fold, eps_occ, eps_vir, kconserve, plan):
    at = jnp.transpose(amps, (0, 2, 3, 1))[0]
    pair = jnp.transpose(ints_pair, (0, 3, 2, 1))
    vmem = pl.BlockSpec(memory_space=pltpu.VMEM)
    smem = pl.BlockSpec(memory_space=pltpu.SMEM)
    x, rows, left, right = pl.pallas_call(
        prep_kernel,
        out_shape=(
            jax.ShapeDtypeStruct((TILES, 2, 16, 128), BF16),
            jax.ShapeDtypeStruct((2, 10, 128, 256), BF16),
            jax.ShapeDtypeStruct((10, 128, 128), F32),
            jax.ShapeDtypeStruct((2, 24, 128), F32),
        ),
        in_specs=[smem, smem] + [vmem] * 5,
        out_specs=(vmem,) * 4,
        compiler_params=pltpu.CompilerParams(vmem_limit_bytes=32 * 2**20),
        name="prep",
    )(plan, kconserve, at, pair, ints_fold, eps_occ.T, eps_vir)
    dma = pltpu.SemaphoreType.DMA
    out = pl.pallas_call(
        main_kernel,
        out_shape=jax.ShapeDtypeStruct((10, 160, 120), BF16),
        in_specs=[smem] + [vmem] * 4,
        out_specs=vmem,
        scratch_shapes=[
            pltpu.VMEM((32, 2, 16, 128), BF16),
            pltpu.VMEM((2, 2, 8, 4, 8, 16, 128), BF16),
            pltpu.VMEM((1280, 256), BF16),
            pltpu.VMEM((1280, 256), BF16),
            pltpu.VMEM((2, 5, 256, 256), F32),
            dma((32,)), dma((32,)),
            dma((8,)), dma((8,)),
            dma((2, 4)), dma((2, 4)),
            dma((2, 4, 2, 2)), dma((2, 4, 2, 2)),
            dma((2, 8, 2)), dma((2, 8, 2)),
        ],
        compiler_params=pltpu.CompilerParams(
            vmem_limit_bytes=40 * 2**20, collective_id=0, has_side_effects=True),
        name="triples",
    )(plan, x, rows, left, right)
    return jnp.transpose(out, (2, 0, 1))[None]


def solution(mesh):
    return jax.shard_map(
        local,
        mesh=mesh,
        in_specs=(
            P("kb", None, "vir", None),
            P("kb", None, None, "vir"),
            P("kb", None, None, None),
            P(),
            P(),
            P(),
            P(),
        ),
        out_specs=P("kb", None, "vir", None),
        check_vma=False,
    )
```

time: 669 us -> 87.6 us (0.13)
  the two profiles are of different devices: /device:TPU:8 before, /device:TPU:1 now
where the time goes in v1:
time: 87.6 us; the launch traced here: 87.2 us
  Pallas kernels  79.8 us (91%)
  local copies, waits for them, and re-layouts  7.37 us (8%)
    pallas_call x1, Pallas kernels, local(): pl.pallas_call(main_kernel, out_shape=jax.ShapeDtypeStruct((10, 160, 120)...  76.8 us
    unnamed x17, local copies, waits for them, and re-layouts  7.37 us
    pallas_call x1, Pallas kernels, local(): pl.pallas_call(prep_kernel, out_shape=(jax.ShapeDtypeStruct((TILES, 2, 16...  3.02 us

profile of v1, /device:TPU:1, one launch (start us, length us, event | category | flops | bytes accessed | tf_op | source)
XLA Modules:
  0.0 87.2 jit_solution(9948750058443854242)
XLA Ops:
  0.0 0.0 copy-start.7
  0.0 0.0 copy-start
  0.0 1.8 %copy-done = bf16[2,16,160,160]{3,2,1,0:T(8,128)(2,1)S(1)} copy-done((bf16[2,16,160,160]{3,2,1,0:T(8,128)(2,1)S(1)}, bf16[2,16,160,160]{3,2,1,0:T(8,128)(2,1)}, u32[]{:S(2)}) %copy-start) | copy-done | bytes 1638424
  1.8 0.0 copy-start.1
  1.8 1.0 %copy-done.1 = bf16[1,120,10,160]{1,3,2,0:T(8,128)(2,1)S(1)} copy-done((bf16[1,120,10,160]{1,3,2,0:T(8,128)(2,1)S(1)}, bf16[1,120,10,160]{1,3,2,0:T(8,128)(2,1)}, u32[]{:S(2)}) %copy-start.1) | copy-done | bytes 384024
  2.8 0.0 copy-start.2
  2.8 0.9 %copy-done.2 = bf16[2,160,16,10]{1,2,3,0:T(8,128)(2,1)S(1)} copy-done((bf16[2,160,16,10]{1,2,3,0:T(8,128)(2,1)S(1)}, bf16[2,160,16,10]{1,2,3,0:T(8,128)(2,1)}, u32[]{:S(2)}) %copy-start.2) | copy-done | bytes 102424
  3.7 0.0 copy-start.3
  3.7 0.8 copy-done.3
  4.5 0.0 copy-start.4
  4.5 0.8 copy-done.4
  5.3 0.0 copy-start.5
  5.3 0.7 copy-done.5
  6.0 0.0 copy-start.6
  6.0 0.7 copy-done.6
  6.6 3.0 %prep.1 = (bf16[25,2,16,128]{3,2,1,0:T(8,128)(2,1)S(1)}, bf16[2,10,128,256]{3,2,1,0:T(8,128)(2,1)S(1)}, f32[10,128,128]{2,1,0:T(8,128)S(1)}, f32[2,24,128]{2,1,0:T(8,128)S(1)}) custom-call(s32[2]{0:T(128)S(1)} %copy-done.6, s32[64,64]{1,0:T(8,128)S(1)} %copy-done.4, bf16[10,160,120]{2,1,0:T(8,128)(2,1)S(1)} %bitcast.9, ...), custom_call_target="tpu_custom_call" | custom-call | tf_op jit(solution)/shard_map/prep/pallas_call | solution.py:326
  9.7 0.0 copy-done.7
  9.7 76.8 %triples.1 = bf16[10,160,120]{2,1,0:T(8,128)(2,1)S(1)} custom-call(s32[2]{0:T(128)S(1)} %copy-done.7, bf16[25,2,16,128]{3,2,1,0:T(8,128)(2,1)S(1)} %get-tuple-element.9.x, bf16[2,10,128,256]{3,2,1,0:T(8,128)(2,1)S(1)} %get-tuple-element.10.l_ref, f32[10,128,128]{2,1,0:T(8,128)S(1)} %get-tuple-element.11.left, f32[2,24,128]{2,1,0:T(8,128)S(1)} %get-tuple-element.12.right), custom_call_target="tpu_custom_call" | custom-call | tf_op jit(solution)/shard_map/triples/pallas_call | solution.py:340
  86.4 0.8 copy.9
Async XLA Ops:
  0.0 9.7 %copy-start.7 = (s32[2]{0:T(128)S(1)}, s32[2]{0:T(128)}, u32[]{:S(2)}) copy-start(s32[2]{0:T(128)} %plan.3) | copy-start | bytes 28
  0.0 1.8 %copy-start = (bf16[2,16,160,160]{3,2,1,0:T(8,128)(2,1)S(1)}, bf16[2,16,160,160]{3,2,1,0:T(8,128)(2,1)}, u32[]{:S(2)}) copy-start(bf16[2,16,160,160]{3,2,1,0:T(8,128)(2,1)} %fold.1) | copy-start | bytes 4915204
  1.8 1.0 %copy-start.1 = (bf16[1,120,10,160]{1,3,2,0:T(8,128)(2,1)S(1)}, bf16[1,120,10,160]{1,3,2,0:T(8,128)(2,1)}, u32[]{:S(2)}) copy-start(bf16[1,120,10,160]{1,3,2,0:T(8,128)(2,1)} %param.7) | copy-start | bytes 1152004
  2.8 0.9 %copy-start.2 = (bf16[2,160,16,10]{1,2,3,0:T(8,128)(2,1)S(1)}, bf16[2,160,16,10]{1,2,3,0:T(8,128)(2,1)}, u32[]{:S(2)}) copy-start(bf16[2,160,16,10]{1,2,3,0:T(8,128)(2,1)} %param.8) | copy-start | bytes 307204
  3.7 0.8 copy-start.3
  4.5 0.8 copy-start.4
  5.3 0.7 copy-start.5
  6.0 0.7 copy-start.6

commit v2 on v0

v2 whole, which is shorter than its diff:
```python
import functools

import jax
import jax.numpy as jnp
import numpy as np
from jax import lax
from jax.experimental import pallas as pl
from jax.experimental.pallas import tpu as pltpu
from jax.sharding import PartitionSpec as P

STEPS = 2
TILES = 25
MESH = pl.DeviceIdType.MESH
F32 = jnp.float32
BF16 = jnp.bfloat16
NT = (((1,), (1,)), ((), ()))
TN = (((0,), (0,)), ((), ()))


def iota(shape, dim):
    return lax.broadcasted_iota(jnp.int32, shape, dim)


def onehot(mask):
    return jnp.where(mask, 1.0, 0.0).astype(BF16)


def kernel(plan, kcons, amps_any, pair_any, fold_any, occt_any, evir_any, out,
           amps, pair, fold, occt, evir, x, rows, left, right, cand, buf, pq, fq, acc,
           s0, s1, r1, s2, r2, s4, r4, s5, r5):
    kb = lax.axis_index("kb")
    vir = lax.axis_index("vir")
    z, yl = kb // 4, kb % 4
    xx, yh, core = vir // 4, (vir // 2) % 2, vir % 2
    y = yh * 4 + yl
    f = y + core * (z - y)
    l = z + core * (y - z)
    kfirst = 2 * kb

    def dev(x_, f_, l_):
        y_ = f_ + core * (l_ - f_)
        z_ = l_ + core * (f_ - l_)
        return (z_ * 4 + y_ % 4, (x_ * 2 + y_ // 4) * 2 + core)

    sibling = (kb, vir + 1 - 2 * core)
    rnext = dev(xx, f, (l + 1) % 8)
    lnext = dev(xx, f, (l + 7) % 8)

    low = pl.multiple_of(jnp.minimum(10 * vir // 16 * 16, 128), 16)
    loads = [
        pltpu.make_async_copy(fold_any.at[:, :, pl.ds(low, 32)], fold, s0.at[0]),
        pltpu.make_async_copy(pair_any, pair, s0.at[1]),
        pltpu.make_async_copy(amps_any, amps, s0.at[2]),
        pltpu.make_async_copy(occt_any, occt, s0.at[3]),
        pltpu.make_async_copy(evir_any, evir, s0.at[4]),
    ]
    for c in loads:
        c.start()

    barrier = pltpu.get_barrier_semaphore()

    def greet(d):
        pl.semaphore_signal(barrier, inc=1, device_id=d, device_id_type=MESH)

    def peer(i):
        return (xx + i // 8) % 4, (f + i) % 8

    @pl.loop(1, 32)
    def _(i):
        greet(((kb + i) % 32, vir))

    @pl.loop(1, 32)
    def _(i):
        a, b = peer(i)
        greet(dev(a, b, l))

    greet(rnext)
    greet(lnext)
    greet(sibling)

    pick = onehot(
        (iota((160, 512), 0) % 16 == iota((160, 512), 1) // 32)
        & (iota((160, 512), 1) % 32 + low == 10 * vir + iota((160, 512), 0) // 16)
    )
    row, col = iota((160, 128), 0), iota((160, 128), 1)
    tail = [onehot((row - 128 == col - 32 * j) & (row >= 128)) for j in range(4)]
    dot = functools.partial(jnp.dot, preferred_element_type=F32)
    loads[0].wait()
    loads[1].wait()
    for s in range(STEPS):
        slot = plan[s] % 2
        p = pair[slot].reshape(5, 2, 16, 160)
        g = dot(pick, fold[slot].reshape(512, 160)).astype(BF16).reshape(5, 2, 16, 160)
        parts = [p[:, 0], p[:, 1], g[:, 0], g[:, 1]]
        for j in range(4):
            x[5 * j:5 * j + 5, s] = parts[j][:, :, :128]
        rem = sum(dot(parts[i].reshape(80, 160), tail[j]) for j, i in enumerate((0, 2, 1, 3)))
        x[20:25, s] = rem.astype(BF16).reshape(5, 16, 128)

    pl.semaphore_wait(barrier, 31 + 31 + 2 + 1)

    def remote(src, dst, ss, rs, d):
        return pltpu.make_async_remote_copy(
            src_ref=src, dst_ref=dst, send_sem=ss, recv_sem=rs, device_id=d, device_id_type=MESH)

    def copy1(i, target, slot):
        return remote(x.at[target], cand.at[slot], s1.at[i], r1.at[i], (target, vir))

    @pl.loop(1, 32)
    def _(i):
        target = (kb + i) % 32

        @pl.when(target < TILES)
        def _():
            copy1(i, target, kb).start()

    loads[2].wait()
    rows[...] = jnp.zeros_like(rows)
    for q in range(2):
        e, to = iota((160, 256), 0), iota((160, 256), 1)
        place = onehot(e + jnp.where(e >= 128, 64 * q, 0) == to)
        for a in range(10):
            rows[q, a, :120] = lax.dot_general(amps[a], place, TN, preferred_element_type=F32).astype(BF16)
    loads[3].wait()
    loads[4].wait()
    row, band = iota((128, 16), 0), iota((128, 16), 1)
    member = jnp.zeros((128, 16), jnp.bool_)
    start = 0
    for i in range(16):
        inside = (row >= start) & (row < start + 15 - i)
        member = member | (inside & ((band == i) | (band == i + 1 + row - start)))
        start += 15 - i
    exact = dict(precision=lax.Precision.HIGHEST, preferred_element_type=F32)
    sums = jnp.dot(jnp.where(member, 1.0, 0.0), occt[...], **exact)
    pe = jnp.sum(jnp.where(iota((128, 64), 1) == kfirst, sums, 0.0), axis=1, keepdims=True)
    level = iota((64, 160), 0)
    vrow = jnp.sum(jnp.where(level == kfirst, evir[...], 0.0), axis=0, keepdims=True)
    for a in range(10):
        mine = jnp.sum(jnp.where(iota((1, 160), 1) == 10 * vir + a, vrow, 0.0), axis=1, keepdims=True)
        left[a] = jnp.broadcast_to(mine - pe, (128, 128))
    lane = iota((160, 256), 1)
    v8 = lane // 16 % 8
    v16 = jnp.where(lane < 128, 2 * v8, (v8 % 4 * 2 + v8 // 4) * 2 + 1)
    spread = jnp.where(iota((160, 256), 0) // 10 == v16, 1.0, 0.0)
    occ16 = lax.dot_general(
        occt[...], jnp.where(iota((16, 256), 1) % 16 == iota((16, 256), 0), 1.0, 0.0), TN, **exact)
    for s in range(STEPS):
        k3 = plan[s]
        k2 = kcons[kfirst, k3]
        vs = jnp.sum(jnp.where(level == k2, evir[...], 0.0), axis=0, keepdims=True)
        own = jnp.where(iota((16, 160), 1) % 10 == iota((16, 160), 0), vs, 0.0)
        occ = jnp.sum(jnp.where(iota((64, 256), 0) == k3, occ16, 0.0), axis=0, keepdims=True)
        right[s] = jnp.dot(own, spread, **exact) - occ

    @pl.when(kb < TILES)
    def _():
        cand[kb] = x[kb]

        @pl.loop(1, 32)
        def _(i):
            copy1(i, kb, (kb + 32 - i) % 32).wait_recv()

        for s in range(STEPS):
            buf[core, l, xx, f, s] = cand[plan[s] // 2, s]

    @pl.when(kb >= TILES)
    def _():
        for s in range(STEPS):
            buf[core, l, xx, f, s] = jnp.zeros((16, 128), BF16)

    def copy2(i, a, b):
        here = buf.at[core, l, a, b]
        to = peer(i)
        return remote(here, here, s2.at[i], r2.at[i], dev(*to, l))

    @pl.loop(1, 32)
    def _(i):
        copy2(i, xx, f).start()

    @pl.loop(1, 32)
    def _(i):
        copy2(i, (xx + 4 - i // 8) % 4, (f + 32 - i) % 8).wait_recv()

    def copy4(t, way, part, origin):
        here = buf.at[core, origin, part]
        return remote(here, here, s4.at[t, way, part], r4.at[t, way, part], lnext if way else rnext)

    def copy5(plane, origin, part):
        here = buf.at[plane, origin, part]
        return remote(here, here, s5.at[origin, part], r5.at[origin, part], sibling)

    for part in range(4):
        for way in range(2):
            copy4(0, way, part, l).start()
    for part in range(4):
        copy5(core, l, part).start()
    for t in range(1, 5):
        for part in range(4):
            for way in range(2):
                if t == 4 and way != part // 2:
                    continue
                origin = (l + t) % 8 if way else (l + 8 - t) % 8
                copy4(t - 1, way, part, origin).wait_recv()
                if t < 3 or (t == 3 and way == part // 2):
                    copy4(t, way, part, origin).start()
                copy5(core, origin, part).start()

    for part in range(4):
        @pl.loop(0, 8)
        def _(o, part=part):
            copy5(1 - core, o, part).wait_recv()

    def tiles(s, base):
        got = []
        for plane in range(2):
            for tp in range(5):
                g = base + tp
                zz, ll = g // 4, g % 4
                if plane == 0:
                    got += [buf[0, zz, a, b * 4 + ll, s] for a in range(4) for b in range(2)]
                else:
                    got += [buf[1, b * 4 + ll, a, zz, s] for b in range(2) for a in range(4)]
        return got

    def assemble(s, q):
        for i, tile in enumerate(tiles(s, 5 * q)):
            pq[16 * i:16 * i + 16, :128] = tile
        for i, tile in enumerate(tiles(s, 10 + 5 * q)):
            fq[16 * i:16 * i + 16, :128] = tile
        for i, tile in enumerate(tiles(s, 20)):
            pq[16 * i:16 * i + 16, 128:] = tile
            fq[16 * i:16 * i + 16, 128:] = tile

    def block(s, q, m):
        mine = rows[q, 5 * m:5 * m + 5].reshape(640, 256)
        lf = left[5 * m:5 * m + 5].reshape(640, 128)
        parts = []
        for j in range(5):
            zeta = lax.dot_general(mine, pq[256 * j:256 * j + 256, :], NT, preferred_element_type=F32)
            for i in range(2):
                plane, tp = (2 * j + i) // 5, (2 * j + i) % 5
                t = 2 * tp + q
                den = lf + right[s, t:t + 1, 128 * plane:128 * plane + 128]
                parts.append((zeta[:, 128 * i:128 * i + 128] / den).astype(BF16))
        return jnp.dot(jnp.concatenate(parts, axis=1), fq[...], preferred_element_type=F32)

    for q in range(2):
        assemble(0, q)
        for m in range(2):
            acc[q, m] = block(0, q, m)
    assemble(1, 0)
    for m in range(2):
        acc[0, m] += block(1, 0, m)
    assemble(1, 1)
    row = iota((160, 256), 0)
    back = onehot(row + jnp.where(row >= 128, 32, 0) == iota((160, 256), 1))
    for m in range(2):
        odd = acc[1, m] + block(1, 1, m)
        even = acc[0, m]
        total = jnp.concatenate(
            [even[:, :128] + odd[:, :128], even[:, 128:] + pltpu.roll(odd[:, 128:], 64, 1)], axis=1
        ).astype(BF16)
        done = lax.dot_general(back, total, NT, preferred_element_type=F32).astype(BF16)
        for a in range(5):
            out[5 * m + a] = done[:, 128 * a:128 * a + 120]

    @pl.loop(1, 32)
    def _(i):
        target = (kb + i) % 32

        @pl.when(target < TILES)
        def _():
            copy1(i, target, kb).wait_send()

    @pl.loop(1, 32)
    def _(i):
        copy2(i, xx, f).wait_send()

    for t in range(4):
        for part in range(4):
            for way in range(2):
                if t == 3 and way != part // 2:
                    continue
                origin = (l + t) % 8 if way else (l + 8 - t) % 8
                copy4(t, way, part, origin).wait_send()
    for part in range(4):
        @pl.loop(0, 8)
        def _(o, part=part):
            copy5(core, o, part).wait_send()


def local(amps, ints_pair, ints_fold, eps_occ, eps_vir, kconserve, plan):
    smem = pl.BlockSpec(memory_space=pltpu.SMEM)
    anywhere = pl.BlockSpec(memory_space=pl.ANY)
    dma = pltpu.SemaphoreType.DMA
    out = pl.pallas_call(
        kernel,
        out_shape=jax.ShapeDtypeStruct((10, 160, 120), BF16),
        in_specs=[smem, smem] + [anywhere] * 5,
        out_specs=pl.BlockSpec(memory_space=pltpu.VMEM),
        scratch_shapes=[
            pltpu.VMEM((10, 160, 120), BF16),
            pltpu.VMEM((2, 10, 16, 160), BF16),
            pltpu.VMEM((2, 16, 32, 160), BF16),
            pltpu.VMEM((16, 64), F32),
            pltpu.VMEM((64, 160), F32),
            pltpu.VMEM((TILES, 2, 16, 128), BF16),
            pltpu.VMEM((2, 10, 128, 256), BF16),
            pltpu.VMEM((10, 128, 128), F32),
            pltpu.VMEM((2, 16, 256), F32),
            pltpu.VMEM((32, 2, 16, 128), BF16),
            pltpu.VMEM((2, 8, 4, 8, 2, 16, 128), BF16),
            pltpu.VMEM((1280, 256), BF16),
            pltpu.VMEM((1280, 256), BF16),
            pltpu.VMEM((2, 2, 640, 256), F32),
            dma((5,)),
            dma((32,)), dma((32,)),
            dma((32,)), dma((32,)),
            dma((4, 2, 4)), dma((4, 2, 4)),
            dma((8, 4)), dma((8, 4)),
        ],
        compiler_params=pltpu.CompilerParams(
            vmem_limit_bytes=56 * 2**20, collective_id=0, has_side_effects=True),
        name="triples",
    )(plan, kconserve, jnp.transpose(amps, (0, 2, 3, 1))[0], jnp.transpose(ints_pair, (0, 3, 2, 1)),
      ints_fold, eps_occ.T, eps_vir)
    return jnp.transpose(out, (2, 0, 1))[None]


def solution(mesh):
    return jax.shard_map(
        local,
        mesh=mesh,
        in_specs=(
            P("kb", None, "vir", None),
            P("kb", None, None, "vir"),
            P("kb", None, None, None),
            P(),
            P(),
            P(),
            P(),
        ),
        out_specs=P("kb", None, "vir", None),
        check_vma=False,
    )
```

time: 669 us -> 65.7 us (0.10)
  the two profiles are of different devices: /device:TPU:8 before, /device:TPU:1 now
where the time goes in v2:
time: 65.7 us; the launch traced here: 65.5 us
  Pallas kernels  63.7 us (97%)
  local copies, waits for them, and re-layouts  1.78 us (3%)
    pallas_call x1, Pallas kernels, local(): pl.pallas_call(kernel, out_shape=jax.ShapeDtypeStruct((10, 160, 120), BF1...  63.7 us
    unnamed x1, local copies, waits for them, and re-layouts  1.78 us

profile of v2, /device:TPU:1, one launch (start us, length us, event | category | flops | bytes accessed | tf_op | source)
XLA Modules:
  0.0 65.5 jit_solution(14914311453298187111)
XLA Ops:
  0.0 63.7 %triples.1 = bf16[10,160,120]{2,1,0:T(8,128)(2,1)} custom-call(s32[2]{0:T(128)} %plan.1, s32[64,64]{1,0:T(8,128)} %kcons.1, bf16[10,160,120]{2,1,0:T(8,128)(2,1)} %bitcast.9, bf16[2,10,16,160]{3,2,1,0:T(8,128)(2,1)} %bitcast.10, bf16[2,16,160,160]{3,2,1,0:T(8,128)(2,1)} %fold_any.1, f32[16,64]{1,0:T(8,128)} %bitcast.11, f32[64,160]{1,0:T(8,128)} %evir_any.1), custom_call_target="tpu_custom_call" | custom-call | tf_op jit(solution)/shard_map/triples/pallas_call | solution.py:296
  63.7 1.8 %copy.9 = bf16[1,120,10,160]{1,3,2,0:T(8,128)(2,1)} copy(bf16[1,120,10,160]{1,3,2,0:T(8,128)(2,1)} %bitcast.8) | data formatting | bytes 768000

commit v3 on v0

v3 whole, which is shorter than its diff:
```python
import functools

import jax
import jax.numpy as jnp
import numpy as np
from jax import lax
from jax.experimental import pallas as pl
from jax.experimental.pallas import tpu as pltpu
from jax.sharding import PartitionSpec as P

STEPS = 2
UNITS = 10
MESH = pl.DeviceIdType.MESH
F32 = jnp.float32
BF16 = jnp.bfloat16
NT = (((1,), (1,)), ((), ()))
TN = (((0,), (0,)), ((), ()))


def iota(shape, dim):
    return lax.broadcasted_iota(jnp.int32, shape, dim)


def onehot(mask):
    return jnp.where(mask, 1.0, 0.0).astype(BF16)


def kernel(plan, kcons, amps_any, pair_any, fold_any, occt_any, evir_any, out,
           amps, pair, fold, occt, evir, x, rows, left, right, cand, buf, pq, fq, acc, part_out, part_in,
           s0, s1, r1, s2, r2, s3, r3, s4, r4, s5, r5):
    kb = lax.axis_index("kb")
    vir = lax.axis_index("vir")
    z, yl = kb >> 2, kb & 3
    xx, yh, core = vir >> 2, (vir >> 1) & 1, vir & 1
    y = yh * 4 + yl
    flip = core == 1
    f = jnp.where(flip, z, y)
    l = jnp.where(flip, y, z)
    kfirst = 2 * kb

    def dev(x_, f_, l_):
        y_ = jnp.where(flip, l_, f_)
        z_ = jnp.where(flip, f_, l_)
        return (z_ * 4 + (y_ & 3), x_ * 4 + (y_ >> 2) * 2 + core)

    def holder(t):
        v8 = xx * 2 + yh
        last = t >= 8
        z0 = jnp.where(last, v8, t)
        y0 = (z0 + v8 + jnp.where(last, t - 7, 0)) & 3
        z1 = jnp.where(last, (2 * xx + t - 4) & 7, t)
        y1 = jnp.where(last, xx, t >> 1)
        return jnp.where(flip, z1 * 4 + y1, z0 * 4 + y0)

    def source(u):
        last = u >= 8
        v8 = jnp.where(last, l, u)
        y0 = (v8 & 1) * 4 + ((l + v8 + jnp.where(last, u - 7, 0)) & 3)
        ll = l & 3
        x1 = jnp.where(last, ll, u & 3)
        z1 = jnp.where(last, (2 * ll + u - 4) & 7, 2 * ll + (u >> 2))
        return jnp.where(flip, x1, v8 >> 1), jnp.where(flip, z1, y0)

    v8 = xx * 2 + yh
    gap = (yl - z - v8) & 3
    extra0 = (z == v8) & ((gap == 1) | (gap == 2))
    main0 = gap == 0
    gap1 = (z - 2 * xx - 4) & 7
    extra1 = (xx == yl) & (gap1 < 2)
    main1 = (z >> 1) == yl
    main = jnp.where(flip, main1.astype(jnp.int32), main0.astype(jnp.int32))
    extra = jnp.where(flip, extra1.astype(jnp.int32), extra0.astype(jnp.int32))
    holds = main + extra
    slot_extra = jnp.where(flip, 8 + gap1, 7 + gap)
    slot_main = jnp.where(flip, (z & 1) * 4 + xx, v8)
    slot = jnp.where(main == 1, slot_main, jnp.where(extra == 1, slot_extra, 0))
    column = jnp.where(main == 1, z, jnp.where(extra == 1, slot_extra, 0))

    sibling = (kb, vir + 1 - 2 * core)
    rnext = dev(xx, f, (l + 1) & 7)
    lnext = dev(xx, f, (l + 7) & 7)

    low = pl.multiple_of(jnp.minimum((10 * vir >> 4) << 4, 128), 16)
    loads = [
        pltpu.make_async_copy(fold_any.at[:, :, pl.ds(low, 32)], fold, s0.at[0]),
        pltpu.make_async_copy(pair_any, pair, s0.at[1]),
        pltpu.make_async_copy(amps_any, amps.at[0], s0.at[2]),
        pltpu.make_async_copy(occt_any, occt, s0.at[3]),
        pltpu.make_async_copy(evir_any, evir, s0.at[4]),
    ]
    for c in loads:
        c.start()

    barrier = pltpu.get_barrier_semaphore()

    def greet(d):
        pl.semaphore_signal(barrier, inc=1, device_id=d, device_id_type=MESH)

    @pl.when(holds == 1)
    def _():
        greet(((kb + 16) & 31, vir))

        @pl.loop(1, 32)
        def _(i):
            @pl.when(i != 16)
            def _():
                greet(((kb + 16 + i) & 31, vir))

    @pl.loop(0, UNITS)
    def _(u):
        a, b = source(u)

        @pl.when((a != xx) | (b != f))
        def _():
            greet(dev(a, b, l))

    greet(rnext)
    greet(lnext)
    greet(sibling)

    pick = onehot(
        (iota((160, 512), 0) % 16 == iota((160, 512), 1) // 32)
        & (iota((160, 512), 1) % 32 + low == 10 * vir + iota((160, 512), 0) // 16)
    )
    row, col = iota((160, 128), 0), iota((160, 128), 1)
    tail = [onehot((row - 128 == col - 32 * j) & (row >= 128)) for j in range(4)]
    dot = functools.partial(jnp.dot, preferred_element_type=F32)
    loads[0].wait()
    loads[1].wait()
    rem = None
    for s in range(STEPS):
        at = plan[s] % 2
        p = pair[at]
        g = dot(pick, fold[at].reshape(512, 160)).astype(BF16)
        x[:, 2 * s] = p[:, :, :128]
        x[:, 2 * s + 1] = g[:, :128].reshape(10, 16, 128)
        ends = dot(p.reshape(160, 160), tail[2 * s]) + dot(g, tail[2 * s + 1])
        rem = ends if rem is None else rem + ends
    x[:, 4] = rem.astype(BF16).reshape(10, 16, 128)
    loads[2].wait()

    pl.semaphore_wait(barrier, UNITS - holds + 31 * holds + 2 + 1)

    def remote(src, dst, ss, rs, d):
        return pltpu.make_async_remote_copy(
            src_ref=src, dst_ref=dst, send_sem=ss, recv_sem=rs, device_id=d, device_id_type=MESH)

    def copy1(t, to, origin):
        return remote(x.at[t], cand.at[origin], s1.at[t], r1.at[origin], (to, vir))

    @pl.loop(0, UNITS)
    def _(t):
        to = holder(t)

        @pl.when(to != kb)
        def _():
            copy1(t, to, kb).start()

    swap = remote(amps.at[0], amps.at[1], s3.at[0], r3.at[0], sibling)
    swap.start()

    loads[3].wait()
    loads[4].wait()
    row, band = iota((128, 16), 0), iota((128, 16), 1)
    member = jnp.zeros((128, 16), jnp.bool_)
    start = 0
    for i in range(16):
        inside = (row >= start) & (row < start + 15 - i)
        member = member | (inside & ((band == i) | (band == i + 1 + row - start)))
        start += 15 - i
    exact = dict(precision=lax.Precision.HIGHEST, preferred_element_type=F32)
    sums = jnp.dot(jnp.where(member, 1.0, 0.0), occt[...], **exact)
    pe = jnp.sum(jnp.where(iota((128, 64), 1) == kfirst, sums, 0.0), axis=1, keepdims=True)
    level = iota((64, 160), 0)
    vrow = jnp.sum(jnp.where(level == kfirst, evir[...], 0.0), axis=0, keepdims=True)
    for who in range(2):
        owner = vir + who * (1 - 2 * core)
        for a in range(10):
            mine = jnp.sum(jnp.where(iota((1, 160), 1) == 10 * owner + a, vrow, 0.0), axis=1, keepdims=True)
            left[who, a] = jnp.broadcast_to(mine - pe, (128, 128))
    lane = iota((160, 128), 1)
    w = lane // 16
    v16 = jnp.where(flip, (w % 4 * 2 + w // 4) * 2 + 1, 2 * w)
    spread = jnp.where(iota((160, 128), 0) // 10 == v16, 1.0, 0.0)
    occ16 = lax.dot_general(
        occt[...], jnp.where(iota((16, 128), 1) % 16 == iota((16, 128), 0), 1.0, 0.0), TN, **exact)
    half = iota((1, 128), 1) < 64
    for s in range(STEPS):
        k3 = plan[s]
        k2 = kcons[kfirst, k3]
        vs = jnp.sum(jnp.where(level == k2, evir[...], 0.0), axis=0, keepdims=True)
        own = jnp.where(iota((16, 160), 1) % 10 == iota((16, 160), 0), vs, 0.0)
        occ = jnp.sum(jnp.where(iota((64, 128), 0) == k3, occ16, 0.0), axis=0, keepdims=True)
        table = jnp.dot(own, spread, **exact) - occ
        turned = pltpu.roll(table, 64, 1)
        for o in range(8):
            t = 2 * (o % 4)
            if o < 4:
                both = jnp.where(half, table[t:t + 1], turned[t + 1:t + 2])
            else:
                both = jnp.where(half, turned[t:t + 1], table[t + 1:t + 2])
            right[s, o:o + 1, :] = jnp.where(flip, both, table[o:o + 1])
        right[s, 8:10, :] = table[8:10]

    e, to = iota((160, 256), 0), iota((160, 256), 1)
    places = [onehot(e + jnp.where(e >= 128, 64 * s, 0) == to) for s in range(STEPS)]

    def lay(who):
        for s in range(STEPS):
            for a in range(10):
                rows[s, who, a, :120] = lax.dot_general(
                    amps[who, a], places[s], TN, preferred_element_type=F32).astype(BF16)
                rows[s, who, a, 120:] = jnp.zeros((8, 256), BF16)

    lay(0)

    @pl.when(holds == 1)
    def _():
        cand[kb] = x[column]

        @pl.loop(1, 32)
        def _(i):
            origin = (kb + i) & 31
            copy1(0, kb, origin).wait_recv()

        first, second = plan[0] // 2, plan[1] // 2
        buf[l, slot, 0] = cand[first, 0]
        buf[l, slot, 1] = cand[first, 1]
        buf[l, slot, 2] = cand[second, 2]
        buf[l, slot, 3] = cand[second, 3]
        buf[l, slot, 4] = jnp.where(
            iota((16, 128), 1) < 64, cand[first, 4].astype(F32), cand[second, 4].astype(F32)).astype(BF16)

    def copy2(i, u):
        here = buf.at[l, u]
        return remote(here, here, s2.at[i], r2.at[u], dev((xx + (i >> 3)) & 3, (f + i) & 7, l))

    @pl.when(holds == 1)
    def _():
        @pl.loop(1, 32)
        def _(i):
            copy2(i, slot).start()

    swap.wait_recv()
    lay(1)

    @pl.loop(0, UNITS)
    def _(u):
        a, b = source(u)

        @pl.when((a != xx) | (b != f))
        def _():
            copy2(1, u).wait_recv()

    def copy4(t, way, part, origin):
        here = buf.at[origin, pl.ds(5 * part, 5)]
        return remote(here, here, s4.at[t, way, part], r4.at[t, way, part], lnext if way else rnext)

    def chunk(n, places_of, edge):
        for s in range(STEPS):
            for i, (o, u) in enumerate(places_of):
                at = slice(16 * i, 16 * i + 16)
                pq[n % 2, s, at, :128] = buf[o, u, 2 * s]
                fq[n % 2, s, at, :128] = buf[o, u, 2 * s + 1]
                pq[n % 2, s, at, 128:] = buf[o, u, 4]
                fq[n % 2, s, at, 128:] = buf[o, u, 4]
        for s in range(STEPS):
            ends = edge(s)
            for m in (2, 3, 0, 1):
                mine = rows[s, m // 2, m % 2 * 5:m % 2 * 5 + 5].reshape(640, 256)
                lf = left[m // 2, m % 2 * 5:m % 2 * 5 + 5].reshape(640, 128)
                zeta = lax.dot_general(mine, pq[n % 2, s], NT, preferred_element_type=F32)
                tri = jnp.concatenate(
                    [(zeta[:, 128 * i:128 * i + 128] / (lf + ends[i])).astype(BF16) for i in range(2)], axis=1)
                got = jnp.dot(tri, fq[n % 2, s], preferred_element_type=F32)
                if n == 0:
                    acc[s, m] = got
                else:
                    acc[s, m] += got

    def pair_of(o1, o2):
        return [(o, u) for o in (o1, o2) for u in range(8)], lambda s: [right[s, pl.ds(o, 1), :] for o in (o1, o2)]

    for part in range(2):
        for way in range(2):
            copy4(0, way, part, l).start()
    for t in range(1, 5):
        for part in range(2):
            for way in range(2):
                if t == 4 and way != part:
                    continue
                origin = (l + t) & 7 if way else (l + 8 - t) & 7
                copy4(t - 1, way, part, origin).wait_recv()
                if t < 3 or (t == 3 and way == part):
                    copy4(t, way, part, origin).start()
        if t < 4:
            chunk(t - 1, *pair_of((l + 8 - t) & 7, (l + t) & 7))
    chunk(3, *pair_of(l, (l + 4) & 7))
    chunk(4, [(o, u) for u in (8, 9) for o in range(8)], lambda s: [right[s, 8:9, :], right[s, 9:10, :]])

    row = iota((160, 256), 0)
    back = onehot(row + jnp.where(row >= 128, 32, 0) == iota((160, 256), 1))

    def turn(m):
        even, odd = acc[0, m], acc[1, m]
        total = jnp.concatenate(
            [even[:, :128] + odd[:, :128], even[:, 128:] + pltpu.roll(odd[:, 128:], 64, 1)], axis=1)
        high = total.astype(BF16)
        rest = (total - high.astype(F32)).astype(BF16)
        return [lax.dot_general(back, h, NT, preferred_element_type=F32) for h in (high, rest)]

    def copy5(m):
        return remote(part_out.at[m], part_in.at[m], s5.at[m], r5.at[m], sibling)

    for m in range(2):
        high, rest = turn(2 + m)
        part_out[m, 0] = high.astype(BF16)
        part_out[m, 1] = rest.astype(BF16)
        copy5(m).start()
    for m in range(2):
        high, rest = turn(m)
        copy5(m).wait_recv()
        done = (high + part_in[m, 0].astype(F32) + (rest + part_in[m, 1].astype(F32))).astype(BF16)
        for a in range(5):
            out[5 * m + a] = done[:, 128 * a:128 * a + 120]

    @pl.loop(0, UNITS)
    def _(t):
        to = holder(t)

        @pl.when(to != kb)
        def _():
            copy1(t, to, kb).wait_send()

    @pl.when(holds == 1)
    def _():
        @pl.loop(1, 32)
        def _(i):
            copy2(i, slot).wait_send()

    swap.wait_send()
    for t in range(4):
        for part in range(2):
            for way in range(2):
                if t == 3 and way != part:
                    continue
                origin = (l + t) & 7 if way else (l + 8 - t) & 7
                copy4(t, way, part, origin).wait_send()
    for m in range(2):
        copy5(m).wait_send()


def local(amps, ints_pair, ints_fold, eps_occ, eps_vir, kconserve, plan):
    smem = pl.BlockSpec(memory_space=pltpu.SMEM)
    anywhere = pl.BlockSpec(memory_space=pl.ANY)
    dma = pltpu.SemaphoreType.DMA
    out = pl.pallas_call(
        kernel,
        out_shape=jax.ShapeDtypeStruct((10, 160, 120), BF16),
        in_specs=[smem, smem] + [anywhere] * 5,
        out_specs=pl.BlockSpec(memory_space=pltpu.VMEM),
        scratch_shapes=[
            pltpu.VMEM((2, 10, 160, 120), BF16),
            pltpu.VMEM((2, 10, 16, 160), BF16),
            pltpu.VMEM((2, 16, 32, 160), BF16),
            pltpu.VMEM((16, 64), F32),
            pltpu.VMEM((64, 160), F32),
            pltpu.VMEM((UNITS, 5, 16, 128), BF16),
            pltpu.VMEM((2, 2, 10, 128, 256), BF16),
            pltpu.VMEM((2, 10, 128, 128), F32),
            pltpu.VMEM((2, 16, 128), F32),
            pltpu.VMEM((32, 5, 16, 128), BF16),
            pltpu.VMEM((8, UNITS, 5, 16, 128), BF16),
            pltpu.VMEM((2, 2, 256, 256), BF16),
            pltpu.VMEM((2, 2, 256, 256), BF16),
            pltpu.VMEM((2, 4, 640, 256), F32),
            pltpu.VMEM((2, 2, 160, 640), BF16),
            pltpu.VMEM((2, 2, 160, 640), BF16),
            dma((5,)),
            dma((UNITS,)), dma((32,)),
            dma((32,)), dma((UNITS,)),
            dma((1,)), dma((1,)),
            dma((4, 2, 2)), dma((4, 2, 2)),
            dma((2,)), dma((2,)),
        ],
        compiler_params=pltpu.CompilerParams(
            vmem_limit_bytes=56 * 2**20, collective_id=0, has_side_effects=True),
        name="triples",
    )(plan, kconserve, jnp.transpose(amps, (0, 2, 3, 1))[0], jnp.transpose(ints_pair, (0, 3, 2, 1)),
      ints_fold, eps_occ.T, eps_vir)
    return jnp.transpose(out, (2, 0, 1))[None]


def solution(mesh):
    return jax.shard_map(
        local,
        mesh=mesh,
        in_specs=(
            P("kb", None, "vir", None),
            P("kb", None, None, "vir"),
            P("kb", None, None, None),
            P(),
            P(),
            P(),
            P(),
        ),
        out_specs=P("kb", None, "vir", None),
        check_vma=False,
    )
```

time: 669 us -> 64.8 us (0.10)
  the two profiles are of different devices: /device:TPU:8 before, /device:TPU:1 now
where the time goes in v3:
time: 64.8 us; the launch traced here: 64.5 us
  Pallas kernels  62.7 us (97%)
  local copies, waits for them, and re-layouts  1.78 us (3%)
    pallas_call x1, Pallas kernels, local(): pl.pallas_call(kernel, out_shape=jax.ShapeDtypeStruct((10, 160, 120), BF1...  62.7 us
    unnamed x1, local copies, waits for them, and re-layouts  1.78 us

profile of v3, /device:TPU:1, one launch (start us, length us, event | category | flops | bytes accessed | tf_op | source)
XLA Modules:
  0.0 64.5 jit_solution(9195534741016383670)
XLA Ops:
  0.0 62.7 %triples.1 = bf16[10,160,120]{2,1,0:T(8,128)(2,1)} custom-call(s32[2]{0:T(128)} %plan.1, s32[64,64]{1,0:T(8,128)} %kcons.1, bf16[10,160,120]{2,1,0:T(8,128)(2,1)} %bitcast.9, bf16[2,10,16,160]{3,2,1,0:T(8,128)(2,1)} %bitcast.10, bf16[2,16,160,160]{3,2,1,0:T(8,128)(2,1)} %fold_any.1, f32[16,64]{1,0:T(8,128)} %bitcast.11, f32[64,160]{1,0:T(8,128)} %evir_any.1), custom_call_target="tpu_custom_call" | custom-call | tf_op jit(solution)/shard_map/triples/pallas_call | solution.py:357
  62.8 1.8 %copy.9 = bf16[1,120,10,160]{1,3,2,0:T(8,128)(2,1)} copy(bf16[1,120,10,160]{1,3,2,0:T(8,128)(2,1)} %bitcast.8) | data formatting | bytes 768000

commit v4 on v3

--- a/solution.py
+++ b/solution.py
@@ -27,7 +27,7 @@
 
 def kernel(plan, kcons, amps_any, pair_any, fold_any, occt_any, evir_any, out,
            amps, pair, fold, occt, evir, x, rows, left, right, cand, buf, pq, fq, acc, part_out, part_in,
-           s0, s1, r1, s2, r2, s3, r3, s4, r4, s5, r5):
+           mid, got, s0, s1, r1, s2, r2, s3, r3, s4, r4, s5, r5, s6, r6, s7, r7):
     kb = lax.axis_index("kb")
     vir = lax.axis_index("vir")
     z, yl = kb >> 2, kb & 3
@@ -47,34 +47,19 @@
         v8 = xx * 2 + yh
         last = t >= 8
         z0 = jnp.where(last, v8, t)
-        y0 = (z0 + v8 + jnp.where(last, t - 7, 0)) & 3
-        z1 = jnp.where(last, (2 * xx + t - 4) & 7, t)
+        y0 = (z0 + xx + jnp.where(last, t - 7, 0)) & 3
+        z1 = jnp.where(last, (xx + 4 * t - 30) & 7, (t & 1) * 4 + xx)
         y1 = jnp.where(last, xx, t >> 1)
-        return jnp.where(flip, z1 * 4 + y1, z0 * 4 + y0)
+        return jnp.where(flip, z1, z0), jnp.where(flip, y1, y0)
 
     def source(u):
         last = u >= 8
         v8 = jnp.where(last, l, u)
-        y0 = (v8 & 1) * 4 + ((l + v8 + jnp.where(last, u - 7, 0)) & 3)
+        y0 = (v8 & 1) * 4 + ((l + (v8 >> 1) + jnp.where(last, u - 7, 0)) & 3)
         ll = l & 3
         x1 = jnp.where(last, ll, u & 3)
-        z1 = jnp.where(last, (2 * ll + u - 4) & 7, 2 * ll + (u >> 2))
+        z1 = jnp.where(last, (ll + 4 * u - 30) & 7, u)
         return jnp.where(flip, x1, v8 >> 1), jnp.where(flip, z1, y0)
-
-    v8 = xx * 2 + yh
-    gap = (yl - z - v8) & 3
-    extra0 = (z == v8) & ((gap == 1) | (gap == 2))
-    main0 = gap == 0
-    gap1 = (z - 2 * xx - 4) & 7
-    extra1 = (xx == yl) & (gap1 < 2)
-    main1 = (z >> 1) == yl
-    main = jnp.where(flip, main1.astype(jnp.int32), main0.astype(jnp.int32))
-    extra = jnp.where(flip, extra1.astype(jnp.int32), extra0.astype(jnp.int32))
-    holds = main + extra
-    slot_extra = jnp.where(flip, 8 + gap1, 7 + gap)
-    slot_main = jnp.where(flip, (z & 1) * 4 + xx, v8)
-    slot = jnp.where(main == 1, slot_main, jnp.where(extra == 1, slot_extra, 0))
-    column = jnp.where(main == 1, z, jnp.where(extra == 1, slot_extra, 0))
 
     sibling = (kb, vir + 1 - 2 * core)
     rnext = dev(xx, f, (l + 1) & 7)
@@ -93,26 +78,28 @@
 
     barrier = pltpu.get_barrier_semaphore()
 
+    def far(i):
+        step = (i + 1) >> 1
+        return 4 - jnp.where((i & 1) == 1, step, -step)
+
     def greet(d):
         pl.semaphore_signal(barrier, inc=1, device_id=d, device_id_type=MESH)
 
-    @pl.when(holds == 1)
-    def _():
-        greet(((kb + 16) & 31, vir))
-
-        @pl.loop(1, 32)
-        def _(i):
-            @pl.when(i != 16)
-            def _():
-                greet(((kb + 16 + i) & 31, vir))
-
-    @pl.loop(0, UNITS)
-    def _(u):
-        a, b = source(u)
-
-        @pl.when((a != xx) | (b != f))
-        def _():
-            greet(dev(a, b, l))
+    @pl.loop(1, 4)
+    def _(i):
+        greet((z * 4 + ((yl + i) & 3), vir))
+
+    @pl.loop(0, 7)
+    def _(i):
+        greet((((z + far(i)) & 7) * 4 + yl, vir))
+
+    @pl.loop(1, 4)
+    def _(i):
+        greet(dev((xx + i) & 3, f, l))
+
+    @pl.loop(0, 7)
+    def _(i):
+        greet(dev(xx, (f + far(i)) & 7, l))
 
     greet(rnext)
     greet(lnext)
@@ -139,22 +126,26 @@
     x[:, 4] = rem.astype(BF16).reshape(10, 16, 128)
     loads[2].wait()
 
-    pl.semaphore_wait(barrier, UNITS - holds + 31 * holds + 2 + 1)
+    pl.semaphore_wait(barrier, 3 + 7 + 3 + 7 + 2 + 1)
 
     def remote(src, dst, ss, rs, d):
         return pltpu.make_async_remote_copy(
             src_ref=src, dst_ref=dst, send_sem=ss, recv_sem=rs, device_id=d, device_id_type=MESH)
 
-    def copy1(t, to, origin):
-        return remote(x.at[t], cand.at[origin], s1.at[t], r1.at[origin], (to, vir))
+    def copy1(t, there):
+        return remote(x.at[t], cand.at[yl, t], s1.at[t], r1.at[yl, t], (z * 4 + there, vir))
 
     @pl.loop(0, UNITS)
     def _(t):
-        to = holder(t)
-
-        @pl.when(to != kb)
-        def _():
-            copy1(t, to, kb).start()
+        there = holder(t)[1]
+
+        @pl.when(there != yl)
+        def _():
+            copy1(t, there).start()
+
+        @pl.when(there == yl)
+        def _():
+            cand[yl, t] = x[t]
 
     swap = remote(amps.at[0], amps.at[1], s3.at[0], r3.at[0], sibling)
     swap.start()
@@ -212,49 +203,127 @@
                     amps[who, a], places[s], TN, preferred_element_type=F32).astype(BF16)
                 rows[s, who, a, 120:] = jnp.zeros((8, 256), BF16)
 
+    first, second = plan[0] // 2, plan[1] // 2
+    split = iota((16, 128), 1) < 64
+
+    def copy2(t, there):
+        return remote(mid.at[t], got.at[z, t], s2.at[t], r2.at[z, t], (there * 4 + yl, vir))
+
+    @pl.loop(0, UNITS)
+    def _(t):
+        @pl.when(holder(t)[1] == yl)
+        def _():
+            @pl.loop(1, 4)
+            def _(i):
+                other = (yl + i) & 3
+                remote(x.at[t], cand.at[other, t], s1.at[t], r1.at[other, t], (z * 4 + yl, vir)).wait_recv()
+
+    @pl.loop(0, UNITS)
+    def _(t):
+        there, row_ = holder(t)
+
+        @pl.when(row_ == yl)
+        def _():
+            one, two = first & 3, second & 3
+            mid[t, 0] = cand[one, t, 0]
+            mid[t, 1] = cand[one, t, 1]
+            mid[t, 2] = cand[two, t, 2]
+            mid[t, 3] = cand[two, t, 3]
+            mid[t, 4] = jnp.where(split, cand[one, t, 4].astype(F32), cand[two, t, 4].astype(F32)).astype(BF16)
+
+            @pl.when(there != z)
+            def _():
+                copy2(t, there).start()
+
+            @pl.when(there == z)
+            def _():
+                got[z, t] = mid[t]
+
     lay(0)
 
-    @pl.when(holds == 1)
-    def _():
-        cand[kb] = x[column]
-
-        @pl.loop(1, 32)
-        def _(i):
-            origin = (kb + i) & 31
-            copy1(0, kb, origin).wait_recv()
-
-        first, second = plan[0] // 2, plan[1] // 2
-        buf[l, slot, 0] = cand[first, 0]
-        buf[l, slot, 1] = cand[first, 1]
-        buf[l, slot, 2] = cand[second, 2]
-        buf[l, slot, 3] = cand[second, 3]
-        buf[l, slot, 4] = jnp.where(
-            iota((16, 128), 1) < 64, cand[first, 4].astype(F32), cand[second, 4].astype(F32)).astype(BF16)
-
-    def copy2(i, u):
+    def slot_of(t):
+        u0 = jnp.where(t >= 8, t, xx * 2 + yh)
+        u1 = jnp.where(t >= 8, t, (t & 1) * 4 + xx)
+        return jnp.where(flip, u1, u0)
+
+    def copy3(u, i):
         here = buf.at[l, u]
-        return remote(here, here, s2.at[i], r2.at[u], dev((xx + (i >> 3)) & 3, (f + i) & 7, l))
-
-    @pl.when(holds == 1)
-    def _():
-        @pl.loop(1, 32)
-        def _(i):
-            copy2(i, slot).start()
+        return remote(here, here, s6.at[i, u], r6.at[u], dev((xx + i) & 3, f, l))
+
+    @pl.loop(0, UNITS)
+    def _(t):
+        there, row_ = holder(t)
+
+        @pl.when((row_ == yl) & (there == z))
+        def _():
+            @pl.loop(1, 8)
+            def _(i):
+                other = (z + i) & 7
+                remote(mid.at[t], got.at[other, t], s2.at[t], r2.at[other, t], (z * 4 + yl, vir)).wait_recv()
+
+            one, two = first >> 2, second >> 2
+            u = slot_of(t)
+            buf[l, u, 0] = got[one, t, 0]
+            buf[l, u, 1] = got[one, t, 1]
+            buf[l, u, 2] = got[two, t, 2]
+            buf[l, u, 3] = got[two, t, 3]
+            buf[l, u, 4] = jnp.where(split, got[one, t, 4].astype(F32), got[two, t, 4].astype(F32)).astype(BF16)
+
+            @pl.loop(1, 4)
+            def _(i):
+                copy3(u, 4 - i).start()
+
+    def copy6(u, i):
+        here = buf.at[l, u]
+        return remote(here, here, s7.at[i, u], r7.at[u], dev(xx, (f + i) & 7, l))
+
+    @pl.loop(0, UNITS)
+    def _(u):
+        a, b = source(u)
+
+        @pl.when(b == f)
+        def _():
+            @pl.when(a != xx)
+            def _():
+                copy3(u, 1).wait_recv()
+
+            @pl.loop(0, 7)
+            def _(i):
+                copy6(u, far(i)).start()
 
     swap.wait_recv()
     lay(1)
 
     @pl.loop(0, UNITS)
     def _(u):
-        a, b = source(u)
-
-        @pl.when((a != xx) | (b != f))
-        def _():
-            copy2(1, u).wait_recv()
+        @pl.when(source(u)[1] != f)
+        def _():
+            copy6(u, 1).wait_recv()
 
     def copy4(t, way, part, origin):
         here = buf.at[origin, pl.ds(5 * part, 5)]
         return remote(here, here, s4.at[t, way, part], r4.at[t, way, part], lnext if way else rnext)
+
+    row = iota((160, 256), 0)
+    back = onehot(row + jnp.where(row >= 128, 32, 0) == iota((160, 256), 1))
+
+    def turn(m):
+        even, odd = acc[0, m], acc[1, m]
+        total = jnp.concatenate(
+            [even[:, :128] + odd[:, :128], even[:, 128:] + pltpu.roll(odd[:, 128:], 64, 1)], axis=1)
+        high = total.astype(BF16)
+        rest = (total - high.astype(F32)).astype(BF16)
+        return [lax.dot_general(back, h, NT, preferred_element_type=F32) for h in (high, rest)]
+
+    def copy5(m):
+        return remote(part_out.at[m], part_in.at[m], s5.at[m], r5.at[m], sibling)
+
+    def hand_over():
+        for m in range(2):
+            high, rest = turn(2 + m)
+            part_out[m, 0] = high.astype(BF16)
+            part_out[m, 1] = rest.astype(BF16)
+            copy5(m).start()
 
     def chunk(n, places_of, edge):
         for s in range(STEPS):
@@ -264,19 +333,22 @@
                 fq[n % 2, s, at, :128] = buf[o, u, 2 * s + 1]
                 pq[n % 2, s, at, 128:] = buf[o, u, 4]
                 fq[n % 2, s, at, 128:] = buf[o, u, 4]
-        for s in range(STEPS):
-            ends = edge(s)
-            for m in (2, 3, 0, 1):
-                mine = rows[s, m // 2, m % 2 * 5:m % 2 * 5 + 5].reshape(640, 256)
-                lf = left[m // 2, m % 2 * 5:m % 2 * 5 + 5].reshape(640, 128)
-                zeta = lax.dot_general(mine, pq[n % 2, s], NT, preferred_element_type=F32)
-                tri = jnp.concatenate(
-                    [(zeta[:, 128 * i:128 * i + 128] / (lf + ends[i])).astype(BF16) for i in range(2)], axis=1)
-                got = jnp.dot(tri, fq[n % 2, s], preferred_element_type=F32)
-                if n == 0:
-                    acc[s, m] = got
-                else:
-                    acc[s, m] += got
+        for ms in ((2, 3), (0, 1)):
+            for s in range(STEPS):
+                ends = edge(s)
+                for m in ms:
+                    mine = rows[s, m // 2, m % 2 * 5:m % 2 * 5 + 5].reshape(640, 256)
+                    lf = left[m // 2, m % 2 * 5:m % 2 * 5 + 5].reshape(640, 128)
+                    zeta = lax.dot_general(mine, pq[n % 2, s], NT, preferred_element_type=F32)
+                    tri = jnp.concatenate(
+                        [(zeta[:, 128 * i:128 * i + 128] / (lf + ends[i])).astype(BF16) for i in range(2)], axis=1)
+                    term = jnp.dot(tri, fq[n % 2, s], preferred_element_type=F32)
+                    if n == 0:
+                        acc[s, m] = term
+                    else:
+                        acc[s, m] += term
+            if n == 4 and ms[0] == 2:
+                hand_over()
 
     def pair_of(o1, o2):
         return [(o, u) for o in (o1, o2) for u in range(8)], lambda s: [right[s, pl.ds(o, 1), :] for o in (o1, o2)]
@@ -298,25 +370,6 @@
     chunk(3, *pair_of(l, (l + 4) & 7))
     chunk(4, [(o, u) for u in (8, 9) for o in range(8)], lambda s: [right[s, 8:9, :], right[s, 9:10, :]])
 
-    row = iota((160, 256), 0)
-    back = onehot(row + jnp.where(row >= 128, 32, 0) == iota((160, 256), 1))
-
-    def turn(m):
-        even, odd = acc[0, m], acc[1, m]
-        total = jnp.concatenate(
-            [even[:, :128] + odd[:, :128], even[:, 128:] + pltpu.roll(odd[:, 128:], 64, 1)], axis=1)
-        high = total.astype(BF16)
-        rest = (total - high.astype(F32)).astype(BF16)
-        return [lax.dot_general(back, h, NT, preferred_element_type=F32) for h in (high, rest)]
-
-    def copy5(m):
-        return remote(part_out.at[m], part_in.at[m], s5.at[m], r5.at[m], sibling)
-
-    for m in range(2):
-        high, rest = turn(2 + m)
-        part_out[m, 0] = high.astype(BF16)
-        part_out[m, 1] = rest.astype(BF16)
-        copy5(m).start()
     for m in range(2):
         high, rest = turn(m)
         copy5(m).wait_recv()
@@ -326,17 +379,27 @@
 
     @pl.loop(0, UNITS)
     def _(t):
-        to = holder(t)
-
-        @pl.when(to != kb)
-        def _():
-            copy1(t, to, kb).wait_send()
-
-    @pl.when(holds == 1)
-    def _():
-        @pl.loop(1, 32)
-        def _(i):
-            copy2(i, slot).wait_send()
+        there, row_ = holder(t)
+
+        @pl.when(row_ != yl)
+        def _():
+            copy1(t, row_).wait_send()
+
+        @pl.when((row_ == yl) & (there != z))
+        def _():
+            copy2(t, there).wait_send()
+
+        @pl.when((row_ == yl) & (there == z))
+        def _():
+            @pl.loop(1, 4)
+            def _(i):
+                copy3(slot_of(t), i).wait_send()
+
+        @pl.when(source(t)[1] == f)
+        def _():
+            @pl.loop(1, 8)
+            def _(i):
+                copy6(t, i).wait_send()
 
     swap.wait_send()
     for t in range(4):
@@ -369,19 +432,23 @@
             pltpu.VMEM((2, 2, 10, 128, 256), BF16),
             pltpu.VMEM((2, 10, 128, 128), F32),
             pltpu.VMEM((2, 16, 128), F32),
-            pltpu.VMEM((32, 5, 16, 128), BF16),
+            pltpu.VMEM((4, UNITS, 5, 16, 128), BF16),
             pltpu.VMEM((8, UNITS, 5, 16, 128), BF16),
             pltpu.VMEM((2, 2, 256, 256), BF16),
             pltpu.VMEM((2, 2, 256, 256), BF16),
             pltpu.VMEM((2, 4, 640, 256), F32),
             pltpu.VMEM((2, 2, 160, 640), BF16),
             pltpu.VMEM((2, 2, 160, 640), BF16),
+            pltpu.VMEM((UNITS, 5, 16, 128), BF16),
+            pltpu.VMEM((8, UNITS, 5, 16, 128), BF16),
             dma((5,)),
-            dma((UNITS,)), dma((32,)),
-            dma((32,)), dma((UNITS,)),
+            dma((UNITS,)), dma((4, UNITS)),
+            dma((UNITS,)), dma((8, UNITS)),
             dma((1,)), dma((1,)),
             dma((4, 2, 2)), dma((4, 2, 2)),
             dma((2,)), dma((2,)),
+            dma((4, UNITS)), dma((UNITS,)),
+            dma((8, UNITS)), dma((UNITS,)),
         ],
         compiler_params=pltpu.CompilerParams(
             vmem_limit_bytes=56 * 2**20, collective_id=0, has_side_effects=True),

time: 64.8 us -> 65.2 us (level)
  no operation moved by 1% of the time
where the time goes in v4:
time: 65.2 us; the launch traced here: 64.9 us
  Pallas kernels  63.1 us (97%)
  local copies, waits for them, and re-layouts  1.78 us (3%)
    pallas_call x1, Pallas kernels, local(): pl.pallas_call(kernel, out_shape=jax.ShapeDtypeStruct((10, 160, 120), BF1...  63.1 us
    unnamed x1, local copies, waits for them, and re-layouts  1.78 us

profile of v4, /device:TPU:1, one launch (start us, length us, event | category | flops | bytes accessed | tf_op | source)
XLA Modules:
  0.0 64.9 jit_solution(12575443289397577212)
XLA Ops:
  0.0 63.1 %triples.1 = bf16[10,160,120]{2,1,0:T(8,128)(2,1)} custom-call(s32[2]{0:T(128)} %plan.1, s32[64,64]{1,0:T(8,128)} %kcons.1, bf16[10,160,120]{2,1,0:T(8,128)(2,1)} %bitcast.9, bf16[2,10,16,160]{3,2,1,0:T(8,128)(2,1)} %bitcast.10, bf16[2,16,160,160]{3,2,1,0:T(8,128)(2,1)} %fold_any.1, f32[16,64]{1,0:T(8,128)} %bitcast.11, f32[64,160]{1,0:T(8,128)} %evir_any.1), custom_call_target="tpu_custom_call" | custom-call | tf_op jit(solution)/shard_map/triples/pallas_call | solution.py:420
  63.1 1.8 %copy.9 = bf16[1,120,10,160]{1,3,2,0:T(8,128)(2,1)} copy(bf16[1,120,10,160]{1,3,2,0:T(8,128)(2,1)} %bitcast.8) | data formatting | bytes 768000

commit v5 on v4

--- a/solution.py
+++ b/solution.py
@@ -25,8 +25,8 @@
     return jnp.where(mask, 1.0, 0.0).astype(BF16)
 
 
-def kernel(plan, kcons, amps_any, pair_any, fold_any, occt_any, evir_any, out,
-           amps, pair, fold, occt, evir, x, rows, left, right, cand, buf, pq, fq, acc, part_out, part_in,
+def kernel(plan_any, kcons_any, amps_any, pair_any, fold_any, occt_any, evir_any, out,
+           plan, kcons, amps, pair, fold, occt, evir, x, rows, left, right, cand, buf, pq, fq, acc, part_out, part_in,
            mid, got, s0, s1, r1, s2, r2, s3, r3, s4, r4, s5, r5, s6, r6, s7, r7):
     kb = lax.axis_index("kb")
     vir = lax.axis_index("vir")
@@ -72,6 +72,8 @@
         pltpu.make_async_copy(amps_any, amps.at[0], s0.at[2]),
         pltpu.make_async_copy(occt_any, occt, s0.at[3]),
         pltpu.make_async_copy(evir_any, evir, s0.at[4]),
+        pltpu.make_async_copy(kcons_any, kcons, s0.at[5]),
+        pltpu.make_async_copy(plan_any, plan, s0.at[6]),
     ]
     for c in loads:
         c.start()
@@ -85,21 +87,15 @@
     def greet(d):
         pl.semaphore_signal(barrier, inc=1, device_id=d, device_id_type=MESH)
 
+    @pl.loop(0, 7)
+    def _(i):
+        greet((((z + far(i)) & 7) * 4 + yl, vir))
+        greet(dev(xx, (f + far(i)) & 7, l))
+
     @pl.loop(1, 4)
     def _(i):
         greet((z * 4 + ((yl + i) & 3), vir))
-
-    @pl.loop(0, 7)
-    def _(i):
-        greet((((z + far(i)) & 7) * 4 + yl, vir))
-
-    @pl.loop(1, 4)
-    def _(i):
         greet(dev((xx + i) & 3, f, l))
-
-    @pl.loop(0, 7)
-    def _(i):
-        greet(dev(xx, (f + far(i)) & 7, l))
 
     greet(rnext)
     greet(lnext)
@@ -112,6 +108,7 @@
     row, col = iota((160, 128), 0), iota((160, 128), 1)
     tail = [onehot((row - 128 == col - 32 * j) & (row >= 128)) for j in range(4)]
     dot = functools.partial(jnp.dot, preferred_element_type=F32)
+    loads[6].wait()
     loads[0].wait()
     loads[1].wait()
     rem = None
@@ -152,6 +149,7 @@
 
     loads[3].wait()
     loads[4].wait()
+    loads[5].wait()
     row, band = iota((128, 16), 0), iota((128, 16), 1)
     member = jnp.zeros((128, 16), jnp.bool_)
     start = 0
@@ -301,7 +299,7 @@
             copy6(u, 1).wait_recv()
 
     def copy4(t, way, part, origin):
-        here = buf.at[origin, pl.ds(5 * part, 5)]
+        here = buf.at[origin, pl.ds(2 * part, 2)]
         return remote(here, here, s4.at[t, way, part], r4.at[t, way, part], lnext if way else rnext)
 
     row = iota((160, 256), 0)
@@ -353,17 +351,17 @@
     def pair_of(o1, o2):
         return [(o, u) for o in (o1, o2) for u in range(8)], lambda s: [right[s, pl.ds(o, 1), :] for o in (o1, o2)]
 
-    for part in range(2):
+    for part in range(5):
         for way in range(2):
             copy4(0, way, part, l).start()
     for t in range(1, 5):
-        for part in range(2):
+        for part in range(5):
             for way in range(2):
-                if t == 4 and way != part:
+                if t == 4 and way != part // 3:
                     continue
                 origin = (l + t) & 7 if way else (l + 8 - t) & 7
                 copy4(t - 1, way, part, origin).wait_recv()
-                if t < 3 or (t == 3 and way == part):
+                if t < 3 or (t == 3 and way == part // 3):
                     copy4(t, way, part, origin).start()
         if t < 4:
             chunk(t - 1, *pair_of((l + 8 - t) & 7, (l + t) & 7))
@@ -403,9 +401,9 @@
 
     swap.wait_send()
     for t in range(4):
-        for part in range(2):
+        for part in range(5):
             for way in range(2):
-                if t == 3 and way != part:
+                if t == 3 and way != part // 3:
                     continue
                 origin = (l + t) & 7 if way else (l + 8 - t) & 7
                 copy4(t, way, part, origin).wait_send()
@@ -414,15 +412,16 @@
 
 
 def local(amps, ints_pair, ints_fold, eps_occ, eps_vir, kconserve, plan):
-    smem = pl.BlockSpec(memory_space=pltpu.SMEM)
     anywhere = pl.BlockSpec(memory_space=pl.ANY)
     dma = pltpu.SemaphoreType.DMA
     out = pl.pallas_call(
         kernel,
         out_shape=jax.ShapeDtypeStruct((10, 160, 120), BF16),
-        in_specs=[smem, smem] + [anywhere] * 5,
+        in_specs=[anywhere] * 7,
         out_specs=pl.BlockSpec(memory_space=pltpu.VMEM),
         scratch_shapes=[
+            pltpu.SMEM((2,), jnp.int32),
+            pltpu.SMEM((64, 64), jnp.int32),
             pltpu.VMEM((2, 10, 160, 120), BF16),
             pltpu.VMEM((2, 10, 16, 160), BF16),
             pltpu.VMEM((2, 16, 32, 160), BF16),
@@ -441,11 +440,11 @@
             pltpu.VMEM((2, 2, 160, 640), BF16),
             pltpu.VMEM((UNITS, 5, 16, 128), BF16),
             pltpu.VMEM((8, UNITS, 5, 16, 128), BF16),
-            dma((5,)),
+            dma((7,)),
             dma((UNITS,)), dma((4, UNITS)),
             dma((UNITS,)), dma((8, UNITS)),
             dma((1,)), dma((1,)),
-            dma((4, 2, 2)), dma((4, 2, 2)),
+            dma((4, 2, 5)), dma((4, 2, 5)),
             dma((2,)), dma((2,)),
             dma((4, UNITS)), dma((UNITS,)),
             dma((8, UNITS)), dma((UNITS,)),

time: 65.2 us -> 63.3 us (0.971)
  Pallas kernels: 63.1 us -> 61.4 us
    pallas_call x1, Pallas kernels: 63.1 us -> 61.4 us  [local(): pl.pallas_call(kernel, out_shape=jax.ShapeDtypeStruct((10, 160, 120), BF1...]
where the time goes in v5:
time: 63.3 us; the launch traced here: 63.2 us
  Pallas kernels  61.4 us (97%)
  local copies, waits for them, and re-layouts  1.78 us (3%)
    pallas_call x1, Pallas kernels, local(): pl.pallas_call(kernel, out_shape=jax.ShapeDtypeStruct((10, 160, 120), BF1...  61.4 us
    unnamed x1, local copies, waits for them, and re-layouts  1.78 us

profile of v5, /device:TPU:1, one launch (start us, length us, event | category | flops | bytes accessed | tf_op | source)
XLA Modules:
  0.0 63.2 jit_solution(13922639045337320552)
XLA Ops:
  0.0 61.4 %triples.1 = bf16[10,160,120]{2,1,0:T(8,128)(2,1)} custom-call(s32[2]{0:T(128)} %plan_any.1, s32[64,64]{1,0:T(8,128)} %kcons_any.1, bf16[10,160,120]{2,1,0:T(8,128)(2,1)} %bitcast.9, bf16[2,10,16,160]{3,2,1,0:T(8,128)(2,1)} %bitcast.10, bf16[2,16,160,160]{3,2,1,0:T(8,128)(2,1)} %fold_any.1, f32[16,64]{1,0:T(8,128)} %bitcast.11, f32[64,160]{1,0:T(8,128)} %evir_any.1), custom_call_target="tpu_custom_call" | custom-call | tf_op jit(solution)/shard_map/triples/pallas_call | solution.py:417
  61.4 1.8 %copy.9 = bf16[1,120,10,160]{1,3,2,0:T(8,128)(2,1)} copy(bf16[1,120,10,160]{1,3,2,0:T(8,128)(2,1)} %bitcast.8) | data formatting | bytes 768000

commit v6 on v5

--- a/solution.py
+++ b/solution.py
@@ -27,7 +27,7 @@
 
 def kernel(plan_any, kcons_any, amps_any, pair_any, fold_any, occt_any, evir_any, out,
            plan, kcons, amps, pair, fold, occt, evir, x, rows, left, right, cand, buf, pq, fq, acc, part_out, part_in,
-           mid, got, s0, s1, r1, s2, r2, s3, r3, s4, r4, s5, r5, s6, r6, s7, r7):
+           mid, got, s0, s1, r1, s2, r2, s3, r3, s4, r4, s5, r5, s6, r6, s7, r7, s8, r8):
     kb = lax.axis_index("kb")
     vir = lax.axis_index("vir")
     z, yl = kb >> 2, kb & 3
@@ -64,6 +64,7 @@
     sibling = (kb, vir + 1 - 2 * core)
     rnext = dev(xx, f, (l + 1) & 7)
     lnext = dev(xx, f, (l + 7) & 7)
+    across = dev(xx, f, (l + 4) & 7)
 
     low = pl.multiple_of(jnp.minimum((10 * vir >> 4) << 4, 128), 16)
     loads = [
@@ -97,6 +98,7 @@
         greet((z * 4 + ((yl + i) & 3), vir))
         greet(dev((xx + i) & 3, f, l))
 
+    greet(across)
     greet(rnext)
     greet(lnext)
     greet(sibling)
@@ -123,7 +125,7 @@
     x[:, 4] = rem.astype(BF16).reshape(10, 16, 128)
     loads[2].wait()
 
-    pl.semaphore_wait(barrier, 3 + 7 + 3 + 7 + 2 + 1)
+    pl.semaphore_wait(barrier, 3 + 7 + 3 + 7 + 3 + 1)
 
     def remote(src, dst, ss, rs, d):
         return pltpu.make_async_remote_copy(
@@ -292,15 +294,13 @@
     swap.wait_recv()
     lay(1)
 
-    @pl.loop(0, UNITS)
-    def _(u):
-        @pl.when(source(u)[1] != f)
-        def _():
-            copy6(u, 1).wait_recv()
-
     def copy4(t, way, part, origin):
         here = buf.at[origin, pl.ds(2 * part, 2)]
         return remote(here, here, s4.at[t, way, part], r4.at[t, way, part], lnext if way else rnext)
+
+    def copy8(origin):
+        here = buf.at[origin]
+        return remote(here, here, s8.at[0], r8.at[0], across)
 
     row = iota((160, 256), 0)
     back = onehot(row + jnp.where(row >= 128, 32, 0) == iota((160, 256), 1))
@@ -352,20 +352,25 @@
         return [(o, u) for o in (o1, o2) for u in range(8)], lambda s: [right[s, pl.ds(o, 1), :] for o in (o1, o2)]
 
     for part in range(5):
+        for u in (2 * part, 2 * part + 1):
+            @pl.when(source(u)[1] != f)
+            def _(u=u):
+                copy6(u, 1).wait_recv()
+
         for way in range(2):
             copy4(0, way, part, l).start()
-    for t in range(1, 5):
+    copy8(l).start()
+    for t in range(1, 4):
+        if t == 3:
+            copy8((l + 4) & 7).wait_recv()
+            chunk(2, *pair_of(l, (l + 4) & 7))
         for part in range(5):
             for way in range(2):
-                if t == 4 and way != part // 3:
-                    continue
                 origin = (l + t) & 7 if way else (l + 8 - t) & 7
                 copy4(t - 1, way, part, origin).wait_recv()
-                if t < 3 or (t == 3 and way == part // 3):
+                if t < 3:
                     copy4(t, way, part, origin).start()
-        if t < 4:
-            chunk(t - 1, *pair_of((l + 8 - t) & 7, (l + t) & 7))
-    chunk(3, *pair_of(l, (l + 4) & 7))
+        chunk(t if t == 3 else t - 1, *pair_of((l + 8 - t) & 7, (l + t) & 7))
     chunk(4, [(o, u) for u in (8, 9) for o in range(8)], lambda s: [right[s, 8:9, :], right[s, 9:10, :]])
 
     for m in range(2):
@@ -400,11 +405,10 @@
                 copy6(t, i).wait_send()
 
     swap.wait_send()
-    for t in range(4):
+    copy8(l).wait_send()
+    for t in range(3):
         for part in range(5):
             for way in range(2):
-                if t == 3 and way != part // 3:
-                    continue
                 origin = (l + t) & 7 if way else (l + 8 - t) & 7
                 copy4(t, way, part, origin).wait_send()
     for m in range(2):
@@ -444,10 +448,11 @@
             dma((UNITS,)), dma((4, UNITS)),
             dma((UNITS,)), dma((8, UNITS)),
             dma((1,)), dma((1,)),
-            dma((4, 2, 5)), dma((4, 2, 5)),
+            dma((3, 2, 5)), dma((3, 2, 5)),
             dma((2,)), dma((2,)),
             dma((4, UNITS)), dma((UNITS,)),
             dma((8, UNITS)), dma((UNITS,)),
+            dma((1,)), dma((1,)),
         ],
         compiler_params=pltpu.CompilerParams(
             vmem_limit_bytes=56 * 2**20, collective_id=0, has_side_effects=True),

time: 63.3 us -> 62.2 us (0.983)
  Pallas kernels: 61.4 us -> 60.2 us
    pallas_call x1, Pallas kernels: 61.4 us -> 60.2 us  [local(): pl.pallas_call(kernel, out_shape=jax.ShapeDtypeStruct((10, 160, 120), BF1...]
where the time goes in v6:
time: 62.2 us; the launch traced here: 62 us
  Pallas kernels  60.2 us (97%)
  local copies, waits for them, and re-layouts  1.78 us (3%)
    pallas_call x1, Pallas kernels, local(): pl.pallas_call(kernel, out_shape=jax.ShapeDtypeStruct((10, 160, 120), BF1...  60.2 us
    unnamed x1, local copies, waits for them, and re-layouts  1.78 us

profile of v6, /device:TPU:1, one launch (start us, length us, event | category | flops | bytes accessed | tf_op | source)
XLA Modules:
  0.0 62.0 jit_solution(14045962341023513226)
XLA Ops:
  0.0 60.2 %triples.1 = bf16[10,160,120]{2,1,0:T(8,128)(2,1)} custom-call(s32[2]{0:T(128)} %plan_any.1, s32[64,64]{1,0:T(8,128)} %kcons_any.1, bf16[10,160,120]{2,1,0:T(8,128)(2,1)} %bitcast.9, bf16[2,10,16,160]{3,2,1,0:T(8,128)(2,1)} %bitcast.10, bf16[2,16,160,160]{3,2,1,0:T(8,128)(2,1)} %fold_any.1, f32[16,64]{1,0:T(8,128)} %bitcast.11, f32[64,160]{1,0:T(8,128)} %evir_any.1), custom_call_target="tpu_custom_call" | custom-call | tf_op jit(solution)/shard_map/triples/pallas_call | solution.py:421
  60.2 1.8 %copy.9 = bf16[1,120,10,160]{1,3,2,0:T(8,128)(2,1)} copy(bf16[1,120,10,160]{1,3,2,0:T(8,128)(2,1)} %bitcast.8) | data formatting | bytes 768000

commit v7 on v6

--- a/solution.py
+++ b/solution.py
@@ -420,7 +420,7 @@
     dma = pltpu.SemaphoreType.DMA
     out = pl.pallas_call(
         kernel,
-        out_shape=jax.ShapeDtypeStruct((10, 160, 120), BF16),
+        out_shape=pltpu.VMEM((10, 160, 120), BF16),
         in_specs=[anywhere] * 7,
         out_specs=pl.BlockSpec(memory_space=pltpu.VMEM),
         scratch_shapes=[

time: 62.2 us -> 60.4 us (0.971)
  local copies, waits for them, and re-layouts: 1.78 us -> 0.75 us
  Pallas kernels: 60.2 us -> 59.5 us
    unnamed x1, local copies, waits for them, and re-layouts: 1.78 us -> 0.75 us
    pallas_call x1, Pallas kernels: 60.2 us -> 59.5 us  [local(): pl.pallas_call(kernel, out_shape=pltpu.VMEM((10, 160, 120), BF16), in_spe...]
where the time goes in v7:
time: 60.4 us; the launch traced here: 60.3 us
  Pallas kernels  59.5 us (99%)
  local copies, waits for them, and re-layouts  0.75 us (1%)
    pallas_call x1, Pallas kernels, local(): pl.pallas_call(kernel, out_shape=pltpu.VMEM((10, 160, 120), BF16), in_spe...  59.5 us

profile of v7, /device:TPU:1, one launch (start us, length us, event | category | flops | bytes accessed | tf_op | source)
XLA Modules:
  0.0 60.3 jit_solution(958857483431018111)
XLA Ops:
  0.0 59.5 %triples.1 = bf16[10,160,120]{2,1,0:T(8,128)(2,1)S(1)} custom-call(s32[2]{0:T(128)} %plan_any.1, s32[64,64]{1,0:T(8,128)} %kcons_any.1, bf16[10,160,120]{2,1,0:T(8,128)(2,1)} %bitcast.9, bf16[2,10,16,160]{3,2,1,0:T(8,128)(2,1)} %bitcast.10, bf16[2,16,160,160]{3,2,1,0:T(8,128)(2,1)} %fold_any.1, f32[16,64]{1,0:T(8,128)} %bitcast.11, f32[64,160]{1,0:T(8,128)} %evir_any.1), custom_call_target="tpu_custom_call" | custom-call | tf_op jit(solution)/shard_map/triples/pallas_call | solution.py:421
  59.5 0.8 %copy.9 = bf16[1,120,10,160]{1,3,2,0:T(8,128)(2,1)} copy(bf16[1,120,10,160]{1,3,2,0:T(8,128)(2,1)S(1)} %bitcast.8) | data formatting | bytes 768000
